TPU v7x, 256 devices: a whole 4x4x8 slice. The times are simulated.
256 devices in a mesh: fsdp: 32 (over y_hi, z, core), vocab: 8 (over y_lo, x).
Axes of the slice: x: 4, y: 4 (y_hi: 2, y_lo: 2; y = y_hi * 2 + y_lo), z: 8, core: 2. Of those that a mesh axis runs over, the one named last changes fastest.
Arguments:
- resid: bfloat16 [3072, 2304], P('fsdp'), may hold values from -6 to 6
- queries: bfloat16 [3072, 2048], P('fsdp', 'vocab'), may hold values from -8 to 8
- new_keys: bfloat16 [3072, 2048], P('fsdp', 'vocab'), may hold values from -6 to 6
- new_values: bfloat16 [3072, 2048], P('fsdp', 'vocab'), may hold values from -12 to 12
- pool_keys: bfloat16 [2048, 128, 2048], P('fsdp', None, 'vocab'), may hold values from -6 to 6
- pool_values: bfloat16 [2048, 128, 2048], P('fsdp', None, 'vocab'), may hold values from -12 to 12
- page_table: int32 [64, 32], P('fsdp'), may hold values from 0 to 95, as said below
- serve_pages: int32 [32, 32, 1], P('fsdp'), may hold values from 32 to 63, as said below
- cache_lengths: int32 [64], P('fsdp'), may hold values from 512 to 4096
- parents: int32 [64, 48], P('fsdp'), may hold values from 0 to 46, as said below
- out_weight: bfloat16 [2048, 2304], P('vocab'), may hold values from -0.125 to 0.125
- norm_gain: float32 [2304], replicated, may hold values from 0.5 to 1.5
- router: bfloat16 [2304, 8], replicated, may hold values from -0.25 to 0.25
- routes: int32 [3072, 2], P('fsdp'), may hold values from 0 to 7, all different within a row; in each aligned block of 96 rows (0 to 95, 96 to 191, ...) at most 36 rows name the same one
- gate_weight: bfloat16 [8, 2304, 5760], P('vocab', None, 'fsdp'), may hold values from -0.125 to 0.125
- up_weight: bfloat16 [8, 2304, 5760], P('vocab', None, 'fsdp'), may hold values from -0.125 to 0.125
- down_weight: bfloat16 [8, 5760, 2304], P('vocab', 'fsdp'), may hold values from -0.078125 to 0.078125
Outputs:
- hidden_out: bfloat16 [3072, 2304], P('fsdp', 'vocab')
Inputs may be any that keep to these rules, and one draw needn't show every extreme that they name: `page_table`: within the rows of one device every entry appears once; entries below 32 name pages of the device's own pool, entries from 64 on name pages held for it by some device (possibly itself), each of those once; entry 64 + h names the one page that device h holds for it. `serve_pages`: each holding device lists each of its pages from 32 on exactly once. `parents`: node 0 is the root and its own parent; every other node's parent comes before it. `routes`: each row names two different experts; within the rows of one device no expert is named more than 36 times.
All inputs are finite; a program needn't handle non-finite values.
Results may differ from a plain program's by a relative error of at most 0.01.
Values may be sent and summed in bfloat16 or wider, within the bound.
A program may use at most 128 MiB of HBM per device.

v0:
```python
import jax
import jax.numpy as jnp
from jax import lax
from jax.sharding import PartitionSpec as P

HEAD_DIM = 64
CAPACITY = 36


NEGATIVE = -1e30
EPSILON = 1e-05


def tree_reach(parent_rows, tree_nodes):
    positions = jnp.arange(tree_nodes, dtype=jnp.int32)
    linked = (parent_rows[:, :, None] == positions[None, None, :]).astype(jnp.float32)
    reached = jnp.minimum(linked + jnp.eye(tree_nodes, dtype=jnp.float32)[None], 1.0)
    for rounds in range(max(1, tree_nodes.bit_length())):
        reached = jnp.minimum(
            jnp.einsum("rij,rjk->rik", reached, reached, precision=lax.Precision.HIGHEST), 1.0
        )
    return reached > 0.5


def head_scores(query_rows, key_rows):
    return jnp.einsum("rqhd,rkhd->rhqk", query_rows, key_rows, preferred_element_type=jnp.float32)


def head_mix(weights, value_rows):
    return jnp.einsum("rhqk,rkhd->rqhd", weights, value_rows, preferred_element_type=jnp.float32)


def per_device(
    resid,
    queries,
    new_keys,
    new_values,
    pool_keys,
    pool_values,
    page_table,
    serve_pages,
    cache_lengths,
    parents,
    out_weight,
    norm_gain,
    router,
    routes,
    gate_weight,
    up_weight,
    down_weight,
):
    requests, pages_each = page_table.shape
    tree_nodes = parents.shape[1]
    page_rows = pool_keys.shape[1]
    features = pool_keys.shape[2]
    heads_here = features // HEAD_DIM
    cache_span = pages_each * page_rows
    score_scale = HEAD_DIM ** (-0.5)
    shaped = (requests, tree_nodes, heads_here, HEAD_DIM)
    cache_shape = (requests, cache_span, heads_here, HEAD_DIM)
    served_pages = serve_pages.reshape(-1)
    query_rows = queries.reshape(shaped)
    tree_keys = new_keys.reshape(shaped)
    tree_values = new_values.reshape(shaped)
    tree_scores = head_scores(query_rows, tree_keys) * score_scale
    ancestry = tree_reach(parents, tree_nodes)
    tree_scores = jnp.where(ancestry[:, None, :, :], tree_scores, NEGATIVE)
    tree_top = jnp.max(tree_scores, axis=-1)
    received_keys, received_values = (
        lax.all_to_all(pool_keys[served_pages], "fsdp", split_axis=0, concat_axis=0, tiled=True),
        lax.all_to_all(pool_values[served_pages], "fsdp", split_axis=0, concat_axis=0, tiled=True),
    )
    joined_keys = jnp.concatenate([pool_keys, received_keys], axis=0)
    joined_values = jnp.concatenate([pool_values, received_values], axis=0)
    cache_keys = joined_keys[page_table].reshape(cache_shape)
    cache_values = joined_values[page_table].reshape(cache_shape)
    cache_scores = head_scores(query_rows, cache_keys) * score_scale
    visible = (jnp.arange(cache_span, dtype=jnp.int32)[None, :] < cache_lengths[:, None])[
        :, None, None, :
    ]
    cache_scores = jnp.where(visible, cache_scores, NEGATIVE)
    highest = jnp.maximum(jnp.max(cache_scores, axis=-1), tree_top)
    cache_weights = jnp.exp(cache_scores - highest[..., None]).astype(jnp.bfloat16)
    cache_sum = jnp.sum(cache_weights, axis=-1, dtype=jnp.float32)
    cache_part = head_mix(cache_weights, cache_values)
    tree_weights = jnp.exp(tree_scores - highest[..., None]).astype(jnp.bfloat16)
    denominator = cache_sum + jnp.sum(tree_weights, axis=-1, dtype=jnp.float32)
    tree_part = head_mix(tree_weights, tree_values)
    attended = (
        (cache_part + tree_part) / jnp.transpose(denominator, (0, 2, 1))[:, :, :, None]
    ).astype(jnp.bfloat16)
    attended = attended.reshape(requests * tree_nodes, features)
    partial_sums = jnp.dot(attended, out_weight, preferred_element_type=jnp.float32)
    projected = lax.psum(partial_sums, "vocab")
    hidden_mid = resid.astype(jnp.float32) + projected
    normed = (
        hidden_mid
        * lax.rsqrt(jnp.mean(hidden_mid * hidden_mid, axis=-1, keepdims=True) + EPSILON)
        * norm_gain
    ).astype(jnp.bfloat16)
    logits = jnp.dot(normed, router, preferred_element_type=jnp.float32)
    labels = jnp.arange(router.shape[1], dtype=jnp.int32)
    picked = routes[:, :, None] == labels[None, None, :]
    chosen = jnp.sum(jnp.where(picked, logits[:, None, :], 0.0), axis=-1)
    first_gate = 1.0 / (1.0 + jnp.exp(chosen[:, 1] - chosen[:, 0]))
    second_gate = 1.0 / (1.0 + jnp.exp(chosen[:, 0] - chosen[:, 1]))
    gate_table = jnp.where(picked[:, 0], first_gate[:, None], 0.0) + jnp.where(
        picked[:, 1], second_gate[:, None], 0.0
    )
    expert_hits = jnp.any(picked, axis=1).astype(jnp.int32)
    expert_ranks = jnp.cumsum(expert_hits, axis=0, dtype=jnp.int32) - expert_hits
    local_count = gate_weight.shape[0]
    offset = lax.axis_index("vocab") * local_count
    local_hits = lax.dynamic_slice_in_dim(expert_hits, offset, local_count, 1)
    local_ranks = lax.dynamic_slice_in_dim(expert_ranks, offset, local_count, 1)
    local_gates = lax.dynamic_slice_in_dim(gate_table, offset, local_count, 1)
    slot_ids = jnp.arange(CAPACITY, dtype=jnp.int32)
    dispatch = (jnp.transpose(local_hits)[:, None, :] > 0) & (
        jnp.transpose(local_ranks)[:, None, :] == slot_ids[None, :, None]
    )
    send_rows = jnp.einsum(
        "ect,td->ecd", dispatch.astype(jnp.bfloat16), normed, preferred_element_type=jnp.float32
    ).astype(jnp.bfloat16)
    piece_rows = lax.all_gather(send_rows, "fsdp", axis=1, tiled=True)
    gate_proj = jnp.einsum(
        "ecd,edf->ecf", piece_rows, gate_weight, preferred_element_type=jnp.float32
    )
    lifted = jnp.einsum("ecd,edf->ecf", piece_rows, up_weight, preferred_element_type=jnp.float32)
    active = (jax.nn.silu(gate_proj) * lifted).astype(jnp.bfloat16)
    block_rows = local_count * CAPACITY
    model_width = resid.shape[1]
    group_count = block_rows * lax.axis_size("fsdp") // block_rows
    taken = active
    taken = taken.reshape(local_count, group_count, CAPACITY, taken.shape[2])
    expert_out = lax.psum_scatter(
        jnp.einsum(
            "egcf,efd->gecd", taken, down_weight, preferred_element_type=jnp.float32
        ).reshape(block_rows * lax.axis_size("fsdp"), model_width),
        "fsdp",
        scatter_dimension=0,
        tiled=True,
    )
    slot_weights = dispatch.astype(jnp.float32) * jnp.transpose(local_gates)[:, None, :]
    mixture = jnp.einsum(
        "ect,ecd->td",
        slot_weights,
        expert_out.reshape(local_count, CAPACITY, model_width),
        precision=lax.Precision.HIGHEST,
    )
    expert_sum = lax.psum_scatter(
        mixture.astype(jnp.bfloat16), "vocab", scatter_dimension=1, tiled=True
    ).astype(jnp.float32)
    column_count = expert_sum.shape[1]
    own_columns = lax.dynamic_slice_in_dim(
        hidden_mid, lax.axis_index("vocab") * column_count, column_count, 1
    )
    return (own_columns + expert_sum).astype(jnp.bfloat16)


def solution(mesh):
    in_specs = (
        P("fsdp", None),
        P("fsdp", "vocab"),
        P("fsdp", "vocab"),
        P("fsdp", "vocab"),
        P("fsdp", None, "vocab"),
        P("fsdp", None, "vocab"),
        P("fsdp", None),
        P("fsdp", None, None),
        P("fsdp"),
        P("fsdp", None),
        P("vocab", None),
        P(),
        P(),
        P("fsdp", None),
        P("vocab", None, "fsdp"),
        P("vocab", None, "fsdp"),
        P("vocab", "fsdp", None),
    )
    out_specs = P("fsdp", "vocab")
    return jax.shard_map(
        per_device, mesh=mesh, in_specs=in_specs, out_specs=out_specs, check_vma=False
    )
```

profile of v0, /device:TPU:32, one launch (start us, length us, event | category | flops | bytes accessed | tf_op | source)
XLA Modules:
  0.0 558.0 jit_solution(13526227225338568584)
XLA Ops:
  7.3 4.2 gather_fusion.2
  11.5 11.5 %all-to-all-start.1 = ((bf16[32,128,256]{2,1,0:T(8,128)(2,1)}), bf16[32,128,256]{2,1,0:T(8,128)(2,1)S(1)}, u32[]{:S(2)}, u32[]{:S(2)}) async-start(bf16[32,128,256]{2,1,0:T(8,128)(2,1)} %gather_fusion.2), calls=%async_computation.1 | async-start | bytes 4194304 | tf_op jit(solution)/shard_map/all_to_all | solution.py:70
  23.0 4.2 gather_fusion
  27.5 48.5 %all-to-all-done.1 = bf16[32,128,256]{2,1,0:T(8,128)(2,1)S(1)} async-done(((bf16[32,128,256]{2,1,0:T(8,128)(2,1)}), bf16[32,128,256]{2,1,0:T(8,128)(2,1)S(1)}, u32[]{:S(2)}, u32[]{:S(2)}) %all-to-all-start.1) | async-done | bytes 2097184 | tf_op jit(solution)/shard_map/all_to_all | solution.py:70
  77.3 3.8 all-to-all-start
  86.0 6.0 %pad_maximum_fusion = bf16[96,128,256]{2,1,0:T(8,128)(2,1)} fusion(bf16[32,128,256]{2,1,0:T(8,128)(2,1)} %copy-done.3, bf16[64,128,256]{2,1,0:T(8,128)(2,1)} %param.21), kind=kLoop, calls=%fused_computation.9 | loop fusion | flops 3145728 | bytes 12582912 | tf_op jit(solution)/shard_map/concatenate | solution.py:73
  92.0 5.5 gather_fusion.3
  97.6 12.9 %reshape.267 = bf16[2,4096,4,64]{3,2,1,0:T(4,128)(2,1)} reshape(bf16[64,128,256]{2,1,0:T(8,128)(2,1)} %gather_fusion.3) | data formatting | bytes 8388608 | tf_op jit(solution)/shard_map/reshape | solution.py:75
  110.5 6.5 %bitcast_reduce_fusion = (f32[2,4,48]{2,1,0:T(4,128)S(1)}, f32[2,4,4096,48]{2,3,1,0:T(8,128)S(1)}) fusion(bf16[2,4096,4,64]{3,2,1,0:T(4,128)(2,1)} %reshape.267, bf16[2,48,4,64]{3,2,1,0:T(4,128)(2,1)S(1)} %reshape.213, pred[2,4096]{1,0:T(4,128)(4,1)S(1)} %iota_compare_fusion.2), kind=kOutput, calls=%fused_computation.12 | convolution fusion | flops 206044800 | bytes 10544640 | tf_op jit(solution)/shard_map/rqhd,rkhd->rhqk/dot_general | solution.py:26
  120.6 13.1 %all-to-all-done = bf16[32,128,256]{2,1,0:T(8,128)(2,1)S(1)} async-done(((bf16[32,128,256]{2,1,0:T(8,128)(2,1)}), bf16[32,128,256]{2,1,0:T(8,128)(2,1)S(1)}, u32[]{:S(2)}, u32[]{:S(2)}) %all-to-all-start) | async-done | bytes 2097184 | tf_op jit(solution)/shard_map/all_to_all | solution.py:71
  133.7 5.4 pad_maximum_fusion.1
  139.1 5.5 gather_fusion.1
  144.7 12.9 %reshape.266 = bf16[2,4096,4,64]{3,2,1,0:T(4,128)(2,1)} reshape(bf16[64,128,256]{2,1,0:T(8,128)(2,1)} %gather_fusion.1) | data formatting | bytes 8388608 | tf_op jit(solution)/shard_map/reshape | solution.py:76
  157.6 7.2 %fusion.14 = f32[2,48,4,64]{3,1,2,0:T(8,128)S(1)} fusion(bf16[2,4096,4,64]{3,2,1,0:T(4,128)(2,1)} %reshape.266, f32[2,4,4096,48]{2,3,1,0:T(8,128)} %copy-done.2, f32[2,4,48]{2,1,0:T(4,128)S(1)} %max.7), kind=kOutput, calls=%fused_computation.27 | convolution fusion | flops 204472320 | bytes 10585600 | tf_op jit(solution)/shard_map/rhqk,rkhd->rqhd/dot_general | solution.py:30
  167.3 75.8 %all-reduce.4.cloned.1.call-done = f32[96,2304]{1,0:T(8,128)} async-done(((f32[96,2304]{1,0:T(8,128)}), f32[96,2304]{1,0:T(8,128)}) %all-reduce.4.cloned.1.call-update) | async-done | bytes 884752 | tf_op jit(solution)/shard_map/psum | solution.py:94
  247.3 90.9 %all-gather.4.cloned.1.call-done = bf16[32,36,2304]{2,1,0:T(8,128)(2,1)} async-done(((bf16[1,36,2304]{2,1,0:T(8,128)(2,1)}), bf16[32,36,2304]{2,1,0:T(8,128)(2,1)}) %all-gather.4.cloned.1.call-update) | async-done | bytes 5308432 | tf_op jit(solution)/shard_map/all_gather | solution.py:124
  338.2 7.7 %reshape.264 = bf16[1152,2304]{1,0:T(8,128)(2,1)} reshape(bf16[32,36,2304]{2,1,0:T(8,128)(2,1)} %all-gather.4.cloned.1.call-done) | data formatting | bytes 10616832
  346.0 4.5 fusion.21
  352.9 6.1 %convolution_bitcast_fusion = f32[32,1,36,2304]{3,2,0,1:T(8,128)} fusion(bf16[32,36,180]{2,1,0:T(8,128)(2,1)S(1)} %reshape.220, bf16[1,180,2304]{2,1,0:T(8,128)(2,1)S(1)} %copy-done.5), kind=kOutput, calls=%fused_computation.8 | convolution fusion | flops 955514880 | bytes 11860992 | tf_op jit(solution)/shard_map/egcf,efd->gecd/dot_general | solution.py:136
  359.0 10.7 %reshape.222 = f32[1152,2304]{1,0:T(8,128)} reshape(f32[32,1,36,2304]{3,2,0,1:T(8,128)} %convolution_bitcast_fusion) | data formatting | bytes 21233664 | tf_op jit(solution)/shard_map/reshape | solution.py:138
  369.7 87.7 %fusion = f32[40,2304]{1,0:T(8,128)S(1)} fusion(f32[1152,2304]{1,0:T(8,128)} %reshape.222), kind=kCustom, calls=%all-reduce-scatter | all-reduce-scatter fusion | flops 2949121 | bytes 10986496
  463.9 15.8 %collective-permute-done.3 = f32[4,2304]{1,0:T(4,128)S(1)} collective-permute-done((f32[4,2304]{1,0:T(4,128)S(1)}, f32[4,2304]{1,0:T(4,128)S(1)}, u32[]{:S(2)}, u32[]{:S(2)}) %collective-permute-start.3) | collective-permute-done | bytes 36896
  480.4 11.6 %concatenate.8 = f32[164,2304]{1,0:T(8,128)} concatenate(f32[4,2304]{1,0:T(4,128)} %copy-done.13, f32[40,2304]{1,0:T(8,128)S(1)} %collective-permute-done.2, f32[40,2304]{1,0:T(8,128)S(1)} %collective-permute-done.1, f32[40,2304]{1,0:T(8,128)S(1)} %collective-permute-done, f32[40,2304]{1,0:T(8,128)S(1)} %fusion), dimensions={0} | concatenate | bytes 3022848
  495.0 54.8 %reduce-scatter.6.cloned.1.call-done = bf16[288,96]{1,0:T(8,128)(2,1)} async-done(((bf16[2304,96]{1,0:T(8,128)(2,1)}), bf16[288,96]{1,0:T(8,128)(2,1)}) %reduce-scatter.6.cloned.1.call-update) | async-done | bytes 55312
  (104 shorter events, 30.9 us)
Async XLA Ops:
  6.5 158.7 %copy-start = (bf16[256,2304]{1,0:T(8,128)(2,1)S(1)}, bf16[256,2304]{1,0:T(8,128)(2,1)}, u32[]{:S(2)}) copy-start(bf16[256,2304]{1,0:T(8,128)(2,1)} %param.27) | copy-start | bytes 3538948
  7.3 19.9 %copy-start.15 = (s32[2,48]{1,0:T(2,128)S(1)}, s32[2,48]{1,0:T(2,128)}, u32[]{:S(2)}) copy-start(s32[2,48]{1,0:T(2,128)} %param.26) | copy-start | bytes 1156
  11.5 69.7 %copy-start.16 = (s32[2,32]{1,0:T(2,128)S(1)}, s32[2,32]{1,0:T(2,128)}, u32[]{:S(2)}) copy-start(s32[2,32]{1,0:T(2,128)} %param.23) | copy-start | bytes 772
  11.5 69.8 %copy-start.10 = (bf16[96,256]{1,0:T(8,128)(2,1)S(1)}, bf16[96,256]{1,0:T(8,128)(2,1)}, u32[]{:S(2)}) copy-start(bf16[96,256]{1,0:T(8,128)(2,1)} %param.18) | copy-start | bytes 147460
  11.5 64.5 %all-to-all-start.1 = ((bf16[32,128,256]{2,1,0:T(8,128)(2,1)}), bf16[32,128,256]{2,1,0:T(8,128)(2,1)S(1)}, u32[]{:S(2)}, u32[]{:S(2)}) async-start(bf16[32,128,256]{2,1,0:T(8,128)(2,1)} %gather_fusion.2), calls=%async_computation.1 | async-start | bytes 4194304 | tf_op jit(solution)/shard_map/all_to_all | solution.py:70
  23.0 59.4 %copy-start.11 = (bf16[96,256]{1,0:T(8,128)(2,1)S(1)}, bf16[96,256]{1,0:T(8,128)(2,1)}, u32[]{:S(2)}) copy-start(bf16[96,256]{1,0:T(8,128)(2,1)} %param.19) | copy-start | bytes 147460
  23.0 62.9 %copy-start.17 = (s32[2]{0:T(128)S(1)}, s32[2]{0:T(128)}, u32[]{:S(2)}) copy-start(s32[2]{0:T(128)} %param.25) | copy-start | bytes 28
  77.3 56.4 %all-to-all-start = ((bf16[32,128,256]{2,1,0:T(8,128)(2,1)}), bf16[32,128,256]{2,1,0:T(8,128)(2,1)S(1)}, u32[]{:S(2)}, u32[]{:S(2)}) async-start(bf16[32,128,256]{2,1,0:T(8,128)(2,1)} %gather_fusion), calls=%async_computation | async-start | bytes 4194304 | tf_op jit(solution)/shard_map/all_to_all | solution.py:71
  81.1 162.0 %all-reduce.4.cloned.1.call-start = ((), (), s32[]{:S(2)}) async-start(), calls=%async_computation.3 | async-start | bytes 1769472 | tf_op jit(solution)/shard_map/psum | solution.py:94
  110.5 6.5 %copy-start.7 = (f32[2,4,48,48]{2,3,1,0:T(8,128)S(1)}, f32[2,4,48,48]{2,3,1,0:T(8,128)}, u32[]{:S(2)}) copy-start(f32[2,4,48,48]{2,3,1,0:T(8,128)} %get-tuple-element.14) | copy-start | bytes 221188
  157.6 7.3 %copy-start.8 = (f32[2,4,48,48]{2,3,1,0:T(8,128)S(1)}, f32[2,4,48,48]{2,3,1,0:T(8,128)}, u32[]{:S(2)}) copy-start(f32[2,4,48,48]{2,3,1,0:T(8,128)} %get-tuple-element.14) | copy-start | bytes 221188
  157.6 9.1 %copy-start.14 = (s32[96,2]{0,1:T(2,128)S(1)}, s32[96,2]{0,1:T(2,128)}, u32[]{:S(2)}) copy-start(s32[96,2]{0,1:T(2,128)} %param.30) | copy-start | bytes 2308
  157.6 85.5 %copy-start.6 = (bf16[96,2304]{1,0:T(8,128)(2,1)S(1)}, bf16[96,2304]{1,0:T(8,128)(2,1)}, u32[]{:S(2)}) copy-start(bf16[96,2304]{1,0:T(8,128)(2,1)} %param.17) | copy-start | bytes 1327108
  164.8 79.7 %copy-start.9 = (f32[2304]{0:T(1024)S(1)}, f32[2304]{0:T(1024)}, u32[]{:S(2)}) copy-start(f32[2304]{0:T(1024)} %param.28) | copy-start | bytes 27652
  164.8 80.9 %copy-start.18 = (u32[256]{0:T(256)S(1)}, u32[256]{0:T(256)}, u32[]{:S(2)}) copy-start(u32[256]{0:T(256)} %constant.55) | copy-start | bytes 3076
  164.8 82.2 %copy-start.12 = (bf16[2304,8]{0,1:T(8,128)(2,1)S(1)}, bf16[2304,8]{0,1:T(8,128)(2,1)}, u32[]{:S(2)}) copy-start(bf16[2304,8]{0,1:T(8,128)(2,1)} %param.29) | copy-start | bytes 110596
  166.6 171.6 %all-gather.4.cloned.1.call-start = ((), (), s32[]{:S(2)}) async-start(), calls=%async_computation.4 | async-start | bytes 6082560 | tf_op jit(solution)/shard_map/all_gather | solution.py:124
  245.5 304.2 %reduce-scatter.6.cloned.1.call-start = ((), (), s32[]{:S(2)}) async-start(), calls=%async_computation.5 | async-start | bytes 663552
  247.3 98.6 %copy-start.19 = (bf16[1,2304,180]{1,2,0:T(8,128)(2,1)S(1)}, bf16[1,2304,180]{1,2,0:T(8,128)(2,1)}, u32[]{:S(2)}) copy-start(bf16[1,2304,180]{1,2,0:T(8,128)(2,1)} %param.31) | copy-start | bytes 2488324
  369.7 181.8 %copy-start.1 = (bf16[256,2304]{1,0:T(8,128)(2,1)S(1)}, bf16[256,2304]{1,0:T(8,128)(2,1)}, u32[]{:S(2)}) copy-start(bf16[256,2304]{1,0:T(8,128)(2,1)} %param.27) | copy-start | bytes 3538948
  457.4 22.4 %collective-permute-start = (f32[40,2304]{1,0:T(8,128)S(1)}, f32[40,2304]{1,0:T(8,128)S(1)}, u32[]{:S(2)}, u32[]{:S(2)}) collective-permute-start(f32[40,2304]{1,0:T(8,128)S(1)} %fusion), channel_id=1, source_target_pairs={{0,8},{8,16},{16,24},{24,32},{32,40},{40,48},{48,56},{56,64},{64,7... | collective-permute-start | bytes 1105928
  459.3 20.5 %collective-permute-start.1 = (f32[40,2304]{1,0:T(8,128)S(1)}, f32[40,2304]{1,0:T(8,128)S(1)}, u32[]{:S(2)}, u32[]{:S(2)}) collective-permute-start(f32[40,2304]{1,0:T(8,128)S(1)} %fusion), channel_id=1, source_target_pairs={{0,16},{8,24},{16,32},{24,40},{32,48},{40,56},{48,64},{56,72},{64,... | collective-permute-start | bytes 1105928
  461.2 19.1 %collective-permute-start.2 = (f32[40,2304]{1,0:T(8,128)S(1)}, f32[40,2304]{1,0:T(8,128)S(1)}, u32[]{:S(2)}, u32[]{:S(2)}) collective-permute-start(f32[40,2304]{1,0:T(8,128)S(1)} %fusion), channel_id=1, source_target_pairs={{0,24},{8,32},{16,40},{24,48},{32,56},{40,64},{48,72},{56,80},{64,... | collective-permute-start | bytes 1105928
  462.6 17.2 %collective-permute-start.3 = (f32[4,2304]{1,0:T(4,128)S(1)}, f32[4,2304]{1,0:T(4,128)S(1)}, u32[]{:S(2)}, u32[]{:S(2)}) collective-permute-start(f32[4,2304]{1,0:T(4,128)S(1)} %slice.28), channel_id=1, source_target_pairs={{0,32},{8,40},{16,48},{24,56},{32,64},{40,72},{48,80},{56,88},{64,... | collective-permute-start | bytes 110600
  (6 other events, 16.1 us)
Sparse Core Ops, SparseCore 0:
  166.7 76.3 all-reduce.3
  246.2 92.0 all-gather.3
  495.1 54.6 reduce-scatter.5
where the time goes:
time: 560 us; the launch traced here: 558 us
  waiting for transfers between devices  299 us (53%)
  blocking collectives  87.7 us (16%)
  local copies, waits for them, and re-layouts  85.3 us (15%)
  matrix products  33.8 us (6%)
  starting transfers between devices  22 us (4%)
  other arithmetic  16 us (3%)
  between operations  14.2 us (3%)
    all_gather x1, waiting for transfers between devices, per_device(): piece_rows = lax.all_gather(send_rows, 'fsdp', axis=1, tiled=True)  90.9 us
    unnamed x1, blocking collectives  87.7 us
    psum x1, waiting for transfers between devices, per_device(): projected = lax.psum(partial_sums, 'vocab')  75.8 us
    unnamed x8, waiting for transfers between devices  70.7 us
    all_to_all x1, waiting for transfers between devices, per_device(): lax.all_to_all(pool_keys[served_pages], 'fsdp', split_axis=0, concat_axis...  48.5 us
    unnamed x48, local copies, waits for them, and re-layouts  26.6 us
    all_to_all x1, waiting for transfers between devices, per_device(): lax.all_to_all(pool_values[served_pages], 'fsdp', split_axis=0, concat_ax...  13.1 us
    reshape x1, local copies, waits for them, and re-layouts, per_device(): cache_values = joined_values[page_table].reshape(cache_shape)  12.9 us
  transfers between devices with their start and end apart: 9, of which 6 were waited for; matrix products, arithmetic and copies ran while one was open for 8% of the time, Pallas kernels for 0%

commit v1 on v0

v1 whole, which is shorter than its diff:
```python
import functools

import jax
import jax.numpy as jnp
from jax import lax
from jax.experimental import pallas as pl
from jax.experimental.pallas import tpu as pltpu
from jax.sharding import PartitionSpec as P

HEAD_DIM = 64
CAPACITY = 36
NEGATIVE = -1e30
EPSILON = 1e-05
MESH = pl.DeviceIdType.MESH
F32 = jnp.float32
BF16 = jnp.bfloat16


def mm(a, b):
    return jnp.dot(a, b, preferred_element_type=F32)


def mm_nt(a, b):
    return lax.dot_general(a, b, (((1,), (1,)), ((), ())), preferred_element_type=F32)


def mm_tn(a, b):
    return lax.dot_general(a, b, (((0,), (0,)), ((), ())), preferred_element_type=F32)


def iota(shape, dim):
    return lax.broadcasted_iota(jnp.int32, shape, dim)


def attention_kernel(
    fs, vs,
    q_ref, nk_ref, nv_ref, table_ref, length_ref, serve_ref, parent_ref, resid_ref, ow_ref, gain_ref,
    pk_ref, pv_ref, wg_ref, wu_ref, wd_ref,
    normed_ref, cols_ref, wg2_ref, wu2_ref, wd2_ref,
    kbuf, vbuf, s_scr, lim_scr, rq_scr, wt_scr, qsend, qrecv, msend, mrecv, osend, orecv, tsend, trecv,
    pown, psend, precv, hsend,
    local_sem, w_sem, q_sem, m_sem, o_sem, t_sem, p_sem, n_sem, h_sem,
):
    requests, pages_each = table_ref.shape
    tree = parent_ref.shape[1]
    features = q_ref.shape[1]
    heads = features // HEAD_DIM
    page_rows = pk_ref.shape[1]
    local_pages = pk_ref.shape[0] // 2
    pool_pages = pk_ref.shape[0]
    rows = heads * tree
    wide = 256
    width = ow_ref.shape[1]
    owners = resid_ref.shape[0]
    me = lax.axis_index("fsdp")
    ve = lax.axis_index("vocab")
    twin = me + 1 - 2 * lax.rem(me, 2)

    barrier = pltpu.get_barrier_semaphore()

    def hail_fsdp(k, carry):
        pl.semaphore_signal(barrier, inc=1, device_id={"fsdp": lax.rem(me + k, fs)}, device_id_type=MESH)
        return carry

    def hail_vocab(k, carry):
        pl.semaphore_signal(barrier, inc=1, device_id={"vocab": lax.rem(ve + k, vs)}, device_id_type=MESH)
        return carry

    lax.fori_loop(1, fs, hail_fsdp, 0)
    lax.fori_loop(1, vs, hail_vocab, 0)
    half = local_pages
    pool_copies = [
        pltpu.make_async_copy(src.at[pl.ds(at, half)], dst.at[pl.ds(at, half)], local_sem.at[i])
        for i, (src, dst, at) in enumerate(
            ((pk_ref, kbuf, 0), (pv_ref, vbuf, 0), (pk_ref, kbuf, half), (pv_ref, vbuf, half))
        )
    ]
    for copy in pool_copies:
        copy.start()

    lane = iota((local_pages, pages_each), 1)
    sub = iota((local_pages, pages_each), 0)
    counts = [jnp.clip(length_ref[r] - page_rows * lane, 0, page_rows) for r in range(requests)]

    def lookup(target):
        hits = [table_ref[r : r + 1, :] == target for r in range(requests)]
        seen = [jnp.sum(jnp.where(h, c, 0).astype(F32), axis=1, keepdims=True) for h, c in zip(hits, counts)]
        return seen, jnp.sum(jnp.where(hits[1], 1.0, 0.0), axis=1, keepdims=True)

    (seen0, seen1), _ = lookup(sub)
    lane_w = iota((local_pages, 2 * wide), 1)
    lim_scr[...] = jnp.where(lane_w < wide, seen0, seen1).astype(jnp.int32)
    holder = lax.rem(sub + me, fs)
    (far0, far1), far_rq = lookup(holder + pool_pages)
    rq_scr[...] = jnp.broadcast_to(far_rq, rq_scr.shape)
    msend[...] = jnp.broadcast_to((far0 + far1)[:, :, None], msend.shape)

    pl.semaphore_wait(barrier, fs - 1 + vs - 1)

    q0 = q_ref[0:tree, :].astype(F32)
    q1 = q_ref[tree : 2 * tree, :].astype(F32)

    def q_copy(k, to):
        return pltpu.make_async_remote_copy(
            src_ref=qsend.at[k], dst_ref=qrecv.at[k], send_sem=q_sem.at[0, k], recv_sem=q_sem.at[1, k],
            device_id={"fsdp": to}, device_id_type=MESH)

    def m_copy(k, to):
        return pltpu.make_async_remote_copy(
            src_ref=msend.at[k], dst_ref=mrecv.at[k], send_sem=m_sem.at[0, k], recv_sem=m_sem.at[1, k],
            device_id={"fsdp": to}, device_id_type=MESH)

    def o_copy(k, to):
        return pltpu.make_async_remote_copy(
            src_ref=osend.at[k], dst_ref=orecv.at[k], send_sem=o_sem.at[0, k], recv_sem=o_sem.at[1, k],
            device_id={"fsdp": to}, device_id_type=MESH)

    def t_copy(k, to):
        return pltpu.make_async_remote_copy(
            src_ref=tsend.at[k], dst_ref=trecv.at[k], send_sem=t_sem.at[0, k], recv_sem=t_sem.at[1, k],
            device_id={"fsdp": to}, device_id_type=MESH)

    def pick_query(k):
        pick = rq_scr[pl.ds(k, 1), :]
        return (q0 * (1.0 - pick) + q1 * pick).astype(BF16)

    def send_query(k, carry):
        qsend[k] = pick_query(k)
        to = lax.rem(me + k, fs)
        q_copy(k, to).start()
        m_copy(k, to).start()
        return carry

    lax.fori_loop(1, fs, send_query, 0)
    qrecv[0] = pick_query(0)
    mrecv[0] = msend[0]

    weight_copies = [
        pltpu.make_async_remote_copy(
            src_ref=src, dst_ref=dst, send_sem=w_sem.at[0, i], recv_sem=w_sem.at[1, i],
            device_id={"fsdp": twin}, device_id_type=MESH)
        for i, (src, dst) in enumerate(((wg_ref, wg2_ref), (wu_ref, wu2_ref), (wd_ref, wd2_ref)))
    ]
    for copy in weight_copies:
        copy.start()

    head_of = iota((1, features), 1) // HEAD_DIM
    head_masks = [jnp.where(head_of == h, 1.0, 0.0) for h in range(heads)]
    scaled_masks = [(m * HEAD_DIM**-0.5).astype(BF16) for m in head_masks]

    def spread(q):
        parts = [q * m for m in scaled_masks]
        return jnp.concatenate(parts + [jnp.zeros((wide - rows, features), BF16)], axis=0)

    def gather_heads(o):
        total = o[0:tree] * head_masks[0]
        for h in range(1, heads):
            total = total + o[h * tree : (h + 1) * tree] * head_masks[h]
        return total

    spread_q = [spread(q_ref[r * tree : (r + 1) * tree, :]) for r in range(requests)]
    both_q = jnp.concatenate(spread_q, axis=0)

    eye = jnp.where(iota((tree, tree), 0) == iota((tree, tree), 1), 1.0, 0.0)
    tile_heads = jnp.where(
        (iota((tree, wide), 1) % tree == iota((tree, wide), 0)) & (iota((tree, wide), 1) < rows), 1.0, 0.0
    ).astype(BF16)
    tree_scores = []
    for r in range(requests):
        linked = jnp.where(parent_ref[r : r + 1, :] == iota((tree, tree), 0), 1.0, 0.0)
        reach = jnp.minimum(linked + eye, 1.0)
        for _ in range(tree.bit_length()):
            half_reach = reach.astype(BF16)
            reach = jnp.minimum(mm(half_reach, half_reach), 1.0)
        seen = mm(reach.astype(BF16), tile_heads)
        scores = mm_nt(nk_ref[r * tree : (r + 1) * tree, :], spread_q[r])
        tree_scores.append(jnp.where(seen > 0.5, scores, NEGATIVE))
    top = jnp.concatenate([jnp.max(s, axis=0, keepdims=True) for s in tree_scores], axis=1)

    pool_copies[0].wait()
    key_row = iota((page_rows, 2 * wide), 0)
    chunk = 4

    def score_chunk(c, top):
        for i in range(chunk):
            page = c * chunk + i
            scores = mm_nt(kbuf[page], both_q)
            scores = jnp.where(key_row < lim_scr[pl.ds(page, 1), :], scores, NEGATIVE)
            s_scr[page] = scores
            top = jnp.maximum(top, jnp.max(scores, axis=0, keepdims=True))
        return top

    top = lax.fori_loop(0, local_pages // chunk, score_chunk, top)
    pool_copies[1].wait()

    def mix_chunk(c, carry):
        total, mixed = carry
        at = pl.ds(c * chunk, chunk)
        weights = jnp.exp(s_scr[at].reshape(chunk * page_rows, 2 * wide) - top).astype(BF16)
        total = total + jnp.sum(weights.astype(F32), axis=0, keepdims=True)
        values = vbuf[at].reshape(chunk * page_rows, features)
        return total, mixed + mm_tn(weights, values)

    total, mixed = lax.fori_loop(
        0, local_pages // chunk, mix_chunk,
        (jnp.zeros((1, 2 * wide), F32), jnp.zeros((2 * wide, features), F32)))
    own_top, own_total, own_mix = [], [], []
    for r in range(requests):
        top_r = top[:, r * wide : (r + 1) * wide]
        weights = jnp.exp(tree_scores[r] - top_r).astype(BF16)
        own_top.append(top_r)
        own_total.append(
            total[:, r * wide : (r + 1) * wide] + jnp.sum(weights.astype(F32), axis=0, keepdims=True))
        mix_r = mixed[r * wide : (r + 1) * wide] + mm_tn(weights, nv_ref[r * tree : (r + 1) * tree, :])
        own_mix.append(gather_heads(mix_r))

    pool_copies[2].wait()
    pool_copies[3].wait()
    stat_row = iota((8, 128), 0)
    held_row = iota((page_rows, wide), 0)

    def serve_one(k):
        asker = lax.rem(me - k + fs, fs)
        page = serve_ref[asker]
        limit = mrecv[k][0:1, :]
        limit = jnp.concatenate([limit, limit], axis=1)
        scores = mm_nt(kbuf[page], spread(qrecv[k]))
        scores = jnp.where(held_row < limit.astype(jnp.int32), scores, NEGATIVE)
        best = jnp.max(scores, axis=0, keepdims=True)
        weights = jnp.exp(scores - best).astype(BF16)
        amount = jnp.sum(weights.astype(F32), axis=0, keepdims=True)
        osend[k] = gather_heads(mm_tn(weights, vbuf[page])).astype(BF16)
        tsend[k] = jnp.where(
            stat_row == 0, best[:, 0:128],
            jnp.where(stat_row == 1, best[:, 128:256],
                      jnp.where(stat_row == 2, amount[:, 0:128], amount[:, 128:256])))

    group = 4

    def serve_group(first):
        base = first * group
        for i in range(group):
            k = base + i

            @pl.when(k > 0)
            def _():
                q_copy(k, me).wait_recv()
                m_copy(k, me).wait_recv()

        for i in range(group):
            serve_one(base + i)
        for i in range(group):
            k = base + i

            @pl.when(k > 0)
            def _():
                to = lax.rem(me - k + fs, fs)
                o_copy(k, to).start()
                t_copy(k, to).start()

    def serve_step(first, carry):
        serve_group(first)
        return carry

    lax.fori_loop(0, fs // group, serve_step, 0)
    orecv[0] = osend[0]
    trecv[0] = tsend[0]

    def await_stats(k, carry):
        t_copy(k, me).wait_recv()
        return carry

    lax.fori_loop(1, fs, await_stats, 0)

    pick = rq_scr[:, 0:128]
    weight_any = [jnp.zeros((fs, 128), F32), jnp.zeros((fs, 128), F32)]
    own_weight = []
    for r in range(requests):
        chosen = pick if r == 1 else 1.0 - pick
        shares = []
        for hh in range(2):
            best = jnp.where(chosen > 0.5, trecv[:, hh, :], NEGATIVE)
            amount = trecv[:, 2 + hh, :]
            mine = own_top[r][:, hh * 128 : (hh + 1) * 128]
            highest = jnp.maximum(jnp.max(best, axis=0, keepdims=True), mine)
            weights = jnp.exp(best - highest) * chosen
            own = jnp.exp(mine - highest)
            bottom = jnp.sum(weights * amount, axis=0, keepdims=True) + (
                own * own_total[r][:, hh * 128 : (hh + 1) * 128])
            weight_any[hh] = weight_any[hh] + weights / bottom
            shares.append(own / bottom)
        own_weight.append(shares)
    for hh in range(2):
        sheet = jnp.concatenate(
            [weight_any[hh]]
            + [jnp.broadcast_to(own_weight[r][hh], (8, 128)) for r in range(requests)]
            + [jnp.zeros((128 - fs - 8 * requests, 128), F32)], axis=0)
        wt_scr[hh * 128 : (hh + 1) * 128, :] = sheet.T

    def factor(col):
        out = wt_scr[0:tree, col : col + 1] * head_masks[0]
        for h in range(1, heads):
            out = out + wt_scr[h * tree : (h + 1) * tree, col : col + 1] * head_masks[h]
        return out

    def await_parts(k, carry):
        o_copy(k, me).wait_recv()
        return carry

    lax.fori_loop(1, fs, await_parts, 0)
    merged = [own_mix[r] * factor(fs + 8 * r) for r in range(requests)]
    for k in range(fs):
        part = orecv[k].astype(F32) * factor(k)
        pick_row = rq_scr[k : k + 1, :]
        merged[0] = merged[0] + part * (1.0 - pick_row)
        merged[1] = merged[1] + part * pick_row
    attended = jnp.concatenate(merged, axis=0).astype(BF16)

    per_owner = resid_ref.shape[1]
    tile = 256
    for c in range(width // tile):
        block = mm(attended, ow_ref[:, c * tile : (c + 1) * tile])
        for o in range(owners):
            piece = block[o * per_owner : (o + 1) * per_owner]
            pown[o, :, c * tile : (c + 1) * tile] = piece
            psend[o, :, c * tile : (c + 1) * tile] = piece.astype(BF16)

    def p_copy(k, to):
        return pltpu.make_async_remote_copy(
            src_ref=psend.at[to], dst_ref=precv.at[k], send_sem=p_sem.at[0, k], recv_sem=p_sem.at[1, k],
            device_id={"vocab": to}, device_id_type=MESH)

    def n_copy(k, owner, to):
        return pltpu.make_async_remote_copy(
            src_ref=normed_ref.at[owner], dst_ref=normed_ref.at[owner],
            send_sem=n_sem.at[0, k], recv_sem=n_sem.at[1, k],
            device_id={"vocab": to}, device_id_type=MESH)

    def h_copy(k, owner, to):
        return pltpu.make_async_remote_copy(
            src_ref=hsend.at[to], dst_ref=cols_ref.at[owner], send_sem=h_sem.at[0, k], recv_sem=h_sem.at[1, k],
            device_id={"vocab": to}, device_id_type=MESH)

    for k in range(1, vs):
        to = lax.rem(ve + k, vs)

        @pl.when(to < owners)
        def _():
            p_copy(k, to).start()

    @pl.when(ve < owners)
    def _():
        hidden = resid_ref[ve].astype(F32) + pown[ve]
        for k in range(1, vs):
            p_copy(k, ve).wait_recv()
            hidden = hidden + precv[k].astype(F32)
        mean = jnp.mean(hidden * hidden, axis=-1, keepdims=True)
        normed_ref[ve] = (hidden * lax.rsqrt(mean + EPSILON) * gain_ref[...]).astype(BF16)
        for k in range(1, vs):
            n_copy(k, ve, lax.rem(ve + k, vs)).start()
        columns = width // vs
        padded = hsend.shape[2]
        for v in range(vs):
            turned = hidden if v == 0 else pltpu.roll(hidden, width - v * columns, 1)
            hsend[v] = turned[:, 0:padded]
        for k in range(1, vs):
            h_copy(k, ve, lax.rem(ve + k, vs)).start()
        cols_ref[ve] = hsend[ve]

    for k in range(1, vs):
        owner = lax.rem(ve - k + vs, vs)

        @pl.when(owner < owners)
        def _():
            n_copy(k, owner, ve).wait_recv()
            h_copy(k, owner, ve).wait_recv()

    def await_sends(k, carry):
        q_copy(k, me).wait_send()
        m_copy(k, me).wait_send()
        o_copy(k, me).wait_send()
        t_copy(k, me).wait_send()
        return carry

    lax.fori_loop(1, fs, await_sends, 0)
    for k in range(1, vs):
        to = lax.rem(ve + k, vs)

        @pl.when(to < owners)
        def _():
            p_copy(k, to).wait_send()

    @pl.when(ve < owners)
    def _():
        for k in range(1, vs):
            to = lax.rem(ve + k, vs)
            n_copy(k, ve, to).wait_send()
            h_copy(k, ve, to).wait_send()

    for copy in weight_copies:
        copy.wait()


def expert_kernel(
    fs, vs, zs,
    normed_ref, cols_ref, routes_ref, router_ref, wg_ref, wu_ref, wd_ref, wg2_ref, wu2_ref, wd2_ref,
    out_ref,
    wg, wu, wd, xbuf, obuf, sbuf, rbuf, ysend, yrecv, yback, yhome, fsend, frecv,
    w_sem, ag_sem, rs_sem, y_sem, b_sem, f_sem,
):
    tokens, width = normed_ref.shape
    pair = xbuf.shape[1]
    block = pair // 2
    slots = ysend.shape[0]
    me = lax.axis_index("fsdp")
    ve = lax.axis_index("vocab")
    core = lax.rem(me, 2)
    z = lax.rem(me // 2, zs)
    yhi = me // (2 * zs)
    right = (yhi * zs + lax.rem(z + 1, zs)) * 2 + core
    left = (yhi * zs + lax.rem(z + zs - 1, zs)) * 2 + core
    across = ((1 - yhi) * zs + z) * 2 + core

    barrier = pltpu.get_barrier_semaphore()
    for peer in (left, right, across):
        pl.semaphore_signal(barrier, inc=1, device_id={"fsdp": peer}, device_id_type=MESH)
    for k in range(1, vs):
        pl.semaphore_signal(barrier, inc=1, device_id={"vocab": lax.rem(ve + k, vs)}, device_id_type=MESH)
    loads = []
    for i, (src, dst) in enumerate(
        ((wg_ref, wg.at[0]), (wg2_ref, wg.at[1]), (wu_ref, wu.at[0]), (wu2_ref, wu.at[1]),
         (wd_ref, wd.at[0]), (wd2_ref, wd.at[1]))):
        loads.append(pltpu.make_async_copy(src, dst, w_sem.at[i]))
    for load in loads:
        load.start()

    lane = iota((tokens, 128), 1)
    first, second = routes_ref[:, 0:1], routes_ref[:, 1:2]
    hits = jnp.where((first == lane) | (second == lane), 1.0, 0.0)
    below = jnp.where(iota((tokens, tokens), 1) < iota((tokens, tokens), 0), 1.0, 0.0).astype(BF16)
    ranks = mm(below, hits.astype(BF16))
    my_hit = jnp.sum(jnp.where(lane == ve, hits, 0.0), axis=1, keepdims=True)
    my_rank = jnp.sum(jnp.where(lane == ve, ranks, 0.0), axis=1, keepdims=True)
    mine = jnp.where((my_hit > 0.5) & (my_rank == lane.astype(F32)), 1.0, 0.0)
    mine_half = mine.astype(BF16)

    picked = mm_tn(mine_half, normed_ref[...])
    ysend[...] = picked[0:slots].astype(BF16)
    pl.semaphore_wait(barrier, 3 + vs - 1)
    y_out = pltpu.make_async_remote_copy(
        src_ref=ysend, dst_ref=yrecv, send_sem=y_sem.at[0], recv_sem=y_sem.at[1],
        device_id={"fsdp": across}, device_id_type=MESH)
    y_out.start()

    logits = mm(normed_ref[...], router_ref[...])
    lane8 = iota(logits.shape, 1)
    chosen0 = jnp.sum(jnp.where(lane8 == first, logits, 0.0), axis=1, keepdims=True)
    chosen1 = jnp.sum(jnp.where(lane8 == second, logits, 0.0), axis=1, keepdims=True)
    gate0 = 1.0 / (1.0 + jnp.exp(chosen1 - chosen0))
    gate1 = 1.0 / (1.0 + jnp.exp(chosen0 - chosen1))
    my_gate = jnp.where(first == ve, gate0, jnp.where(second == ve, gate1, 0.0))
    slot_gate = jnp.sum((mine * my_gate).T, axis=1, keepdims=True)[0:slots]
    spread_e = jnp.where(iota((128, vs * slots), 0) == iota((128, vs * slots), 1) // slots, 1.0, 0.0).astype(BF16)
    all_hits = mm(hits.astype(BF16), spread_e)
    all_ranks = mm(ranks.astype(BF16), spread_e)
    slot_at = (iota((tokens, vs * slots), 1) % slots).astype(F32)
    back = jnp.where((all_hits > 0.5) & (all_ranks == slot_at), 1.0, 0.0).astype(BF16)

    y_out.wait_recv()
    xbuf[0] = jnp.concatenate([picked[0:block], yrecv[...].astype(F32)[0:block]], axis=0).astype(BF16)

    cut = width // 2
    ways = (right, left)
    steps = zs // 2

    def halves(step, way):
        return (way,) if step == steps - 1 else (0, 1)

    def gather_copy(way, step, h):
        src = 0 if step == 0 else 2 * step - 1 + way
        dst = zs - 1 if step == steps - 1 else 2 * step + 1 + way
        at = pl.ds(h * cut, cut)
        return pltpu.make_async_remote_copy(
            src_ref=xbuf.at[src, :, at], dst_ref=xbuf.at[dst, :, at],
            send_sem=ag_sem.at[0, way, step, h], recv_sem=ag_sem.at[1, way, step, h],
            device_id={"fsdp": ways[way]}, device_id_type=MESH)

    def expert(first_block, count):
        rows = xbuf[first_block : first_block + count].reshape(count * pair, width)
        acts = []
        for j in range(2):
            gate = mm(rows, wg[j])
            acts.append((gate / (1.0 + jnp.exp(-gate)) * mm(rows, wu[j])).astype(BF16))
        tile = width // 3
        for c in range(3):
            at = pl.ds(c * tile, tile)
            out = mm(acts[0], wd[0, :, at]) + mm(acts[1], wd[1, :, at])
            obuf[first_block : first_block + count, :, at] = out.reshape(count, pair, tile)

    for step in range(steps):
        for way in range(2):
            for h in (0, 1):
                if step > 0:
                    gather_copy(way, step - 1, h).wait_recv()
                if h in halves(step, way):
                    gather_copy(way, step, h).start()
        if step == 0:
            for load in loads:
                load.wait()
            expert(0, 1)
        else:
            expert(2 * step - 1, 2)
    for way in range(2):
        gather_copy(way, steps - 1, way).wait_recv()
    expert(zs - 1, 1)

    def sum_copy(way, step, h):
        at = pl.ds(h * cut, cut)
        return pltpu.make_async_remote_copy(
            src_ref=sbuf.at[way, step, :, at], dst_ref=rbuf.at[way, step, :, at],
            send_sem=rs_sem.at[0, way, step, h], recv_sem=rs_sem.at[1, way, step, h],
            device_id={"fsdp": ways[way]}, device_id_type=MESH)

    for step in range(steps):
        for h in (0, 1):
            for way in range(2):
                at = pl.ds(h * cut, cut)
                if step == 0:
                    if h != way:
                        continue
                    sbuf[way, 0, :, at] = obuf[zs - 1, :, at].astype(BF16)
                else:
                    source = 2 * (steps - step) - way
                    value = obuf[source, :, at]
                    if step > 1 or h == way:
                        sum_copy(way, step - 1, h).wait_recv()
                        value = value + rbuf[way, step - 1, :, at].astype(F32)
                    sbuf[way, step, :, at] = value.astype(BF16)
                sum_copy(way, step, h).start()
    for way in range(2):
        for h in (0, 1):
            sum_copy(way, steps - 1, h).wait_recv()
    whole = obuf[0] + rbuf[0, steps - 1].astype(F32) + rbuf[1, steps - 1].astype(F32)
    yback[...] = jnp.concatenate(
        [whole[block:pair], jnp.zeros((slots - block, width), F32)], axis=0).astype(BF16)
    b_out = pltpu.make_async_remote_copy(
        src_ref=yback, dst_ref=yhome, send_sem=b_sem.at[0], recv_sem=b_sem.at[1],
        device_id={"fsdp": across}, device_id_type=MESH)
    b_out.start()
    b_out.wait_recv()
    gated = (whole[0:slots] + yhome[...].astype(F32)) * slot_gate

    columns = width // vs
    padded = fsend.shape[2]

    def f_copy(k, to, slot):
        return pltpu.make_async_remote_copy(
            src_ref=fsend.at[to], dst_ref=frecv.at[slot], send_sem=f_sem.at[0, k], recv_sem=f_sem.at[1, k],
            device_id={"vocab": to}, device_id_type=MESH)

    for v in range(vs):
        turned = gated if v == 0 else pltpu.roll(gated, width - v * columns, 1)
        fsend[v] = turned[:, 0:padded].astype(BF16)
    for k in range(1, vs):
        f_copy(k, lax.rem(ve + k, vs), ve).start()
    frecv[ve] = fsend[ve]
    for k in range(1, vs):
        f_copy(k, ve, lax.rem(ve - k + vs, vs)).wait_recv()
    mixture = mm(back, frecv[...].reshape(vs * slots, padded))
    out_ref[...] = (cols_ref[...] + mixture)[:, 0:columns].astype(BF16)

    y_out.wait_send()
    b_out.wait_send()
    for step in range(steps):
        for way in range(2):
            for h in halves(step, way):
                gather_copy(way, step, h).wait_send()
    for step in range(steps):
        for way in range(2):
            for h in (0, 1):
                if step > 0 or h == way:
                    sum_copy(way, step, h).wait_send()
    for k in range(1, vs):
        f_copy(k, lax.rem(ve + k, vs), ve).wait_send()


def per_device(
    resid, queries, new_keys, new_values, pool_keys, pool_values, page_table, serve_pages, cache_lengths, parents,
    out_weight, norm_gain, router, routes, gate_weight, up_weight, down_weight,
):
    fs, vs = lax.axis_size("fsdp"), lax.axis_size("vocab")
    zs = fs // 4
    tokens, width = resid.shape
    features = queries.shape[1]
    tree = parents.shape[1]
    pool_pages, page_rows, _ = pool_keys.shape
    hidden = gate_weight.shape[2]
    vmem = pl.BlockSpec(memory_space=pltpu.VMEM)
    smem = pl.BlockSpec(memory_space=pltpu.SMEM)
    hbm = pl.BlockSpec(memory_space=pl.ANY)
    dma = pltpu.SemaphoreType.DMA
    padded = -(-(width // vs) // 128) * 128
    per_owner = 16
    owners = tokens // per_owner
    wg, wu, wd = gate_weight[0], up_weight[0], down_weight[0]
    like = lambda a: jax.ShapeDtypeStruct(a.shape, a.dtype)
    normed, cols, wg2, wu2, wd2 = pl.pallas_call(
        functools.partial(attention_kernel, fs, vs),
        out_shape=(
            jax.ShapeDtypeStruct((owners, per_owner, width), BF16),
            jax.ShapeDtypeStruct((owners, per_owner, padded), F32),
            like(wg), like(wu), like(wd)),
        in_specs=[vmem] * 4 + [smem] * 2 + [vmem] * 4 + [hbm] * 5,
        out_specs=(vmem, vmem, hbm, hbm, hbm),
        scratch_shapes=[
            pltpu.VMEM(pool_keys.shape, BF16),
            pltpu.VMEM(pool_values.shape, BF16),
            pltpu.VMEM((pool_pages // 2, page_rows, 512), F32),
            pltpu.VMEM((pool_pages // 2, 512), jnp.int32),
            pltpu.VMEM((fs, features), F32),
            pltpu.VMEM((256, 128), F32),
            pltpu.VMEM((fs, tree, features), BF16),
            pltpu.VMEM((fs, tree, features), BF16),
            pltpu.VMEM((fs, 8, 128), F32),
            pltpu.VMEM((fs, 8, 128), F32),
            pltpu.VMEM((fs, tree, features), BF16),
            pltpu.VMEM((fs, tree, features), BF16),
            pltpu.VMEM((fs, 8, 128), F32),
            pltpu.VMEM((fs, 8, 128), F32),
            pltpu.VMEM((owners, per_owner, width), F32),
            pltpu.VMEM((owners, per_owner, width), BF16),
            pltpu.VMEM((vs, per_owner, width), BF16),
            pltpu.VMEM((vs, per_owner, padded), F32),
            dma((4,)), dma((2, 3)), dma((2, fs)), dma((2, fs)), dma((2, fs)), dma((2, fs)),
            dma((2, vs)), dma((2, vs)), dma((2, vs)),
        ],
        compiler_params=pltpu.CompilerParams(
            collective_id=1, has_side_effects=True, vmem_limit_bytes=56 * 2**20),
        name="attention",
    )(
        queries, new_keys, new_values, page_table, cache_lengths, serve_pages.reshape(-1), parents,
        resid.reshape(owners, per_owner, width), out_weight, norm_gain.reshape(1, width),
        pool_keys, pool_values, wg, wu, wd)
    pair, slots = 80, 48
    return pl.pallas_call(
        functools.partial(expert_kernel, fs, vs, zs),
        out_shape=jax.ShapeDtypeStruct((tokens, width // vs), BF16),
        in_specs=[vmem] * 4 + [hbm] * 6,
        out_specs=vmem,
        scratch_shapes=[
            pltpu.VMEM((2, width, hidden), BF16),
            pltpu.VMEM((2, width, hidden), BF16),
            pltpu.VMEM((2, hidden, width), BF16),
            pltpu.VMEM((zs, pair, width), BF16),
            pltpu.VMEM((zs, pair, width), F32),
            pltpu.VMEM((2, zs // 2, pair, width), BF16),
            pltpu.VMEM((2, zs // 2, pair, width), BF16),
            pltpu.VMEM((slots, width), BF16),
            pltpu.VMEM((slots, width), BF16),
            pltpu.VMEM((slots, width), BF16),
            pltpu.VMEM((slots, width), BF16),
            pltpu.VMEM((vs, slots, padded), BF16),
            pltpu.VMEM((vs, slots, padded), BF16),
            dma((6,)), dma((2, 2, zs // 2, 2)), dma((2, 2, zs // 2, 2)), dma((2,)), dma((2,)), dma((2, vs)),
        ],
        compiler_params=pltpu.CompilerParams(
            collective_id=2, has_side_effects=True, vmem_limit_bytes=56 * 2**20),
        name="experts",
    )(normed.reshape(tokens, width), cols.reshape(tokens, padded), routes, router, wg, wu, wd, wg2, wu2, wd2)


def solution(mesh):
    in_specs = (
        P("fsdp", None), P("fsdp", "vocab"), P("fsdp", "vocab"), P("fsdp", "vocab"),
        P("fsdp", None, "vocab"), P("fsdp", None, "vocab"), P("fsdp", None), P("fsdp", None, None),
        P("fsdp"), P("fsdp", None), P("vocab", None), P(), P(), P("fsdp", None),
        P("vocab", None, "fsdp"), P("vocab", None, "fsdp"), P("vocab", "fsdp", None),
    )
    return jax.shard_map(
        per_device, mesh=mesh, in_specs=in_specs, out_specs=P("fsdp", "vocab"), check_vma=False
    )
```

time: 560 us -> 174 us (0.31)
  waiting for transfers between devices: 299 us -> 0 us
  Pallas kernels: 0 us -> 164 us
  blocking collectives: 87.7 us -> 0 us
  local copies, waits for them, and re-layouts: 85.3 us -> 9.86 us
  matrix products: 33.8 us -> 0 us
  starting transfers between devices: 22 us -> 0 us
  other arithmetic: 16 us -> 0 us
  between operations: 14.2 us -> 0.02 us
    pallas_call x0 -> x2, Pallas kernels: none -> 164 us  [the longest x1 87.2 us: per_device(): pl.pallas_call(functools.partial(expert_kernel, fs, vs, zs), out_shape=ja...]
    all_gather x1 -> x0, waiting for transfers between devices: 90.9 us -> none  [per_device(): piece_rows = lax.all_gather(send_rows, 'fsdp', axis=1, tiled=True)]
    unnamed x1 -> x0, blocking collectives: 87.7 us -> none
    psum x1 -> x0, waiting for transfers between devices: 75.8 us -> none  [per_device(): projected = lax.psum(partial_sums, 'vocab')]
    unnamed x8 -> x0, waiting for transfers between devices: 70.7 us -> none
    all_to_all x2 -> x0, waiting for transfers between devices: 61.6 us -> none  [the longest x1 48.5 us: per_device(): lax.all_to_all(pool_keys[served_pages], 'fsdp', split_axis=0, concat_axis...]
    reshape x7 -> x1, local copies, waits for them, and re-layouts: 38.4 us -> 1.31 us  [per_device(): norm_gain.reshape(1, width)]
    dot_general x17 -> x0, matrix products: 33.8 us -> none  [the longest x2 8.24 us: head_scores(): jnp.einsum('rqhd,rkhd->rhqk', query_rows, key_rows, preferred_element_typ...]
  transfers between devices with their start and end apart: 9 -> 0, of which waited for: 6 -> 0; matrix products, arithmetic and copies ran while one was open for 8% -> 0% of each run, Pallas kernels for 0% -> 0%
where the time goes in v1:
time: 174 us; the launch traced here: 173 us
  Pallas kernels  164 us (94%)
  local copies, waits for them, and re-layouts  9.86 us (6%)
    pallas_call x1, Pallas kernels, per_device(): pl.pallas_call(functools.partial(expert_kernel, fs, vs, zs), out_shape=ja...  87.2 us
    pallas_call x1, Pallas kernels, per_device(): pl.pallas_call(functools.partial(attention_kernel, fs, vs), out_shape=(ja...  76.4 us
    unnamed x7, local copies, waits for them, and re-layouts  8.55 us

profile of v1, /device:TPU:32, one launch (start us, length us, event | category | flops | bytes accessed | tf_op | source)
XLA Modules:
  0.0 173.4 jit_solution(4449894557399755785)
XLA Ops:
  0.0 1.3 reshape.17.gain_ref
  1.3 1.4 copy.20.routes_ref
  2.7 0.0 copy-start
  2.7 1.9 %copy.21.router_ref = bf16[2304,8]{1,0:T(8,128)(2,1)} copy(bf16[2304,8]{0,1:T(8,128)(2,1)} %param.29) | data formatting | bytes 73728 | tf_op args[12]
  4.6 2.3 %copy.18 = bf16[1,2304,180]{2,1,0:T(8,128)(2,1)} copy(bf16[1,2304,180]{1,2,0:T(8,128)(2,1)} %param.31) | data formatting | bytes 1658880 | tf_op args[14]
  6.9 0.0 copy-done
  6.9 1.4 copy.19
  8.3 76.4 %attention.1 = (bf16[6,16,2304]{2,1,0:T(8,128)(2,1)}, f32[6,16,384]{2,1,0:T(8,128)}, bf16[2304,180]{1,0:T(8,128)(2,1)}, bf16[2304,180]{1,0:T(8,128)(2,1)}, bf16[180,2304]{1,0:T(8,128)(2,1)}) custom-call(bf16[96,256]{1,0:T(8,128)(2,1)} %q_ref.1, bf16[96,256]{1,0:T(8,128)(2,1)} %nk_ref.1, bf16[96,256]{1,0:T(8,128)(2,1)} %nv_ref.1, s32[2,32]{1,0:T(2,128)} %table_ref.1, ...), custom_call_target="tpu_custom_call" | custom-call | tf_op jit(solution)/shard_map/attention/pallas_call | solution.py:607
  84.7 87.2 %experts.1 = bf16[96,288]{1,0:T(8,128)(2,1)} custom-call(bf16[96,2304]{1,0:T(8,128)(2,1)} %bitcast.14, f32[96,384]{1,0:T(8,128)} %bitcast.15, s32[96,2]{1,0:T(8,128)} %copy.20.routes_ref, bf16[2304,8]{1,0:T(8,128)(2,1)} %copy.21.router_ref, bf16[2304,180]{1,0:T(8,128)(2,1)} %bitcast.8, bf16[2304,180]{1,0:T(8,128)(2,1)} %bitcast.10, ...), custom_call_target="tpu_custom_call" | custom-call | tf_op jit(solution)/shard_map/experts/pallas_call | solution.py:645
  171.9 1.5 copy.23
Async XLA Ops:
  2.7 4.2 %copy-start = (bf16[1,2304,180]{1,2,0:T(8,128)(2,1)S(1)}, bf16[1,2304,180]{1,2,0:T(8,128)(2,1)}, u32[]{:S(2)}) copy-start(bf16[1,2304,180]{1,2,0:T(8,128)(2,1)} %param.32) | copy-start | bytes 2488324

commit v2 on v1

--- a/solution.py
+++ b/solution.py
@@ -35,8 +35,8 @@
 def attention_kernel(
     fs, vs,
     q_ref, nk_ref, nv_ref, table_ref, length_ref, serve_ref, parent_ref, resid_ref, ow_ref, gain_ref,
-    pk_ref, pv_ref, wg_ref, wu_ref, wd_ref,
-    normed_ref, cols_ref, wg2_ref, wu2_ref, wd2_ref,
+    pk_ref, pv_ref, wg_ref, wu_ref,
+    normed_ref, cols_ref, more_ref,
     kbuf, vbuf, s_scr, lim_scr, rq_scr, wt_scr, qsend, qrecv, msend, mrecv, osend, orecv, tsend, trecv,
     pown, psend, precv, hsend,
     local_sem, w_sem, q_sem, m_sem, o_sem, t_sem, p_sem, n_sem, h_sem,
@@ -55,6 +55,7 @@
     me = lax.axis_index("fsdp")
     ve = lax.axis_index("vocab")
     twin = me + 1 - 2 * lax.rem(me, 2)
+    across = lax.rem(me + fs // 2, fs)
 
     barrier = pltpu.get_barrier_semaphore()
 
@@ -135,13 +136,17 @@
     qrecv[0] = pick_query(0)
     mrecv[0] = msend[0]
 
-    weight_copies = [
-        pltpu.make_async_remote_copy(
-            src_ref=src, dst_ref=dst, send_sem=w_sem.at[0, i], recv_sem=w_sem.at[1, i],
-            device_id={"fsdp": twin}, device_id_type=MESH)
-        for i, (src, dst) in enumerate(((wg_ref, wg2_ref), (wu_ref, wu2_ref), (wd_ref, wd2_ref)))
-    ]
-    for copy in weight_copies:
+    kinds = (wg_ref, wu_ref)
+
+    def weight_copy(src, at, to):
+        return pltpu.make_async_remote_copy(
+            src_ref=src, dst_ref=more_ref.at[at], send_sem=w_sem.at[0, at], recv_sem=w_sem.at[1, at],
+            device_id={"fsdp": to}, device_id_type=MESH)
+
+    far_copies = [weight_copy(src, 2 + i, across) for i, src in enumerate(kinds)]
+    near_copies = [weight_copy(src, i, twin) for i, src in enumerate(kinds)]
+    pass_copies = [weight_copy(more_ref.at[2 + i], 4 + i, twin) for i in range(2)]
+    for copy in far_copies + near_copies:
         copy.start()
 
     head_of = iota((1, features), 1) // HEAD_DIM
@@ -216,13 +221,13 @@
 
     pool_copies[2].wait()
     pool_copies[3].wait()
-    stat_row = iota((8, 128), 0)
+    stat_row = iota((4, 128), 0)
     held_row = iota((page_rows, wide), 0)
 
     def serve_one(k):
         asker = lax.rem(me - k + fs, fs)
         page = serve_ref[asker]
-        limit = mrecv[k][0:1, :]
+        limit = mrecv[k]
         limit = jnp.concatenate([limit, limit], axis=1)
         scores = mm_nt(kbuf[page], spread(qrecv[k]))
         scores = jnp.where(held_row < limit.astype(jnp.int32), scores, NEGATIVE)
@@ -316,6 +321,15 @@
         merged[1] = merged[1] + part * pick_row
     attended = jnp.concatenate(merged, axis=0).astype(BF16)
 
+    side, per_side = vs // 2, owners // 2
+
+    def owns(v):
+        return lax.rem(v, side) < per_side
+
+    def share(v):
+        return v // side * per_side + lax.rem(v, side)
+
+    own = share(ve)
     per_owner = resid_ref.shape[1]
     tile = 256
     for c in range(width // tile):
@@ -327,7 +341,7 @@
 
     def p_copy(k, to):
         return pltpu.make_async_remote_copy(
-            src_ref=psend.at[to], dst_ref=precv.at[k], send_sem=p_sem.at[0, k], recv_sem=p_sem.at[1, k],
+            src_ref=psend.at[share(to)], dst_ref=precv.at[k], send_sem=p_sem.at[0, k], recv_sem=p_sem.at[1, k],
             device_id={"vocab": to}, device_id_type=MESH)
 
     def n_copy(k, owner, to):
@@ -344,36 +358,40 @@
     for k in range(1, vs):
         to = lax.rem(ve + k, vs)
 
-        @pl.when(to < owners)
+        @pl.when(owns(to))
         def _():
             p_copy(k, to).start()
 
-    @pl.when(ve < owners)
+    for far, onward in zip(far_copies, pass_copies):
+        far.wait_recv()
+        onward.start()
+
+    @pl.when(owns(ve))
     def _():
-        hidden = resid_ref[ve].astype(F32) + pown[ve]
+        hidden = resid_ref[own].astype(F32) + pown[own]
         for k in range(1, vs):
             p_copy(k, ve).wait_recv()
             hidden = hidden + precv[k].astype(F32)
         mean = jnp.mean(hidden * hidden, axis=-1, keepdims=True)
-        normed_ref[ve] = (hidden * lax.rsqrt(mean + EPSILON) * gain_ref[...]).astype(BF16)
+        normed_ref[own] = (hidden * lax.rsqrt(mean + EPSILON) * gain_ref[...].reshape(1, width)).astype(BF16)
         for k in range(1, vs):
-            n_copy(k, ve, lax.rem(ve + k, vs)).start()
+            n_copy(k, own, lax.rem(ve + k, vs)).start()
         columns = width // vs
         padded = hsend.shape[2]
         for v in range(vs):
             turned = hidden if v == 0 else pltpu.roll(hidden, width - v * columns, 1)
             hsend[v] = turned[:, 0:padded]
         for k in range(1, vs):
-            h_copy(k, ve, lax.rem(ve + k, vs)).start()
-        cols_ref[ve] = hsend[ve]
+            h_copy(k, own, lax.rem(ve + k, vs)).start()
+        cols_ref[own] = hsend[ve]
 
     for k in range(1, vs):
         owner = lax.rem(ve - k + vs, vs)
 
-        @pl.when(owner < owners)
+        @pl.when(owns(owner))
         def _():
-            n_copy(k, owner, ve).wait_recv()
-            h_copy(k, owner, ve).wait_recv()
+            n_copy(k, share(owner), ve).wait_recv()
+            h_copy(k, share(owner), ve).wait_recv()
 
     def await_sends(k, carry):
         q_copy(k, me).wait_send()
@@ -386,32 +404,37 @@
     for k in range(1, vs):
         to = lax.rem(ve + k, vs)
 
-        @pl.when(to < owners)
+        @pl.when(owns(to))
         def _():
             p_copy(k, to).wait_send()
 
-    @pl.when(ve < owners)
+    @pl.when(owns(ve))
     def _():
         for k in range(1, vs):
             to = lax.rem(ve + k, vs)
-            n_copy(k, ve, to).wait_send()
-            h_copy(k, ve, to).wait_send()
-
-    for copy in weight_copies:
+            n_copy(k, own, to).wait_send()
+            h_copy(k, own, to).wait_send()
+
+    for copy in far_copies:
+        copy.wait_send()
+    for copy in near_copies + pass_copies:
         copy.wait()
 
 
 def expert_kernel(
     fs, vs, zs,
-    normed_ref, cols_ref, routes_ref, router_ref, wg_ref, wu_ref, wd_ref, wg2_ref, wu2_ref, wd2_ref,
+    normed_ref, cols_ref, routes_ref, router_ref, wg_ref, wu_ref, wd_ref, more_ref,
     out_ref,
-    wg, wu, wd, xbuf, obuf, sbuf, rbuf, ysend, yrecv, yback, yhome, fsend, frecv,
-    w_sem, ag_sem, rs_sem, y_sem, b_sem, f_sem,
+    wraw, weights, rt_scr, xbuf, obuf, sbuf, rbuf, fsend, frecv,
+    w_sem, d_sem, ag_sem, rs_sem, f_sem,
 ):
     tokens, width = normed_ref.shape
-    pair = xbuf.shape[1]
-    block = pair // 2
-    slots = ysend.shape[0]
+    block = xbuf.shape[1] // 2
+    cut = xbuf.shape[2]
+    slots = fsend.shape[1]
+    kinds, sources = 3, wraw.shape[0] // 3
+    hidden = wraw.shape[1]
+    pitch = weights.shape[1]
     me = lax.axis_index("fsdp")
     ve = lax.axis_index("vocab")
     core = lax.rem(me, 2)
@@ -419,112 +442,142 @@
     yhi = me // (2 * zs)
     right = (yhi * zs + lax.rem(z + 1, zs)) * 2 + core
     left = (yhi * zs + lax.rem(z + zs - 1, zs)) * 2 + core
-    across = ((1 - yhi) * zs + z) * 2 + core
+    twin = me + 1 - 2 * core
+    across = lax.rem(me + fs // 2, fs)
 
     barrier = pltpu.get_barrier_semaphore()
-    for peer in (left, right, across):
+    for peer in (left, right, twin, across):
         pl.semaphore_signal(barrier, inc=1, device_id={"fsdp": peer}, device_id_type=MESH)
     for k in range(1, vs):
         pl.semaphore_signal(barrier, inc=1, device_id={"vocab": lax.rem(ve + k, vs)}, device_id_type=MESH)
     loads = []
-    for i, (src, dst) in enumerate(
-        ((wg_ref, wg.at[0]), (wg2_ref, wg.at[1]), (wu_ref, wu.at[0]), (wu2_ref, wu.at[1]),
-         (wd_ref, wd.at[0]), (wd2_ref, wd.at[1]))):
-        loads.append(pltpu.make_async_copy(src, dst, w_sem.at[i]))
+    for i, src in enumerate((wg_ref, wu_ref, wd_ref)):
+        loads.append(pltpu.make_async_copy(src, wraw.at[i * sources], w_sem.at[i * sources]))
+        for j in range(1, sources if i < 2 else 1):
+            loads.append(pltpu.make_async_copy(
+                more_ref.at[(j - 1) * 2 + i], wraw.at[i * sources + j], w_sem.at[i * sources + j]))
     for load in loads:
         load.start()
 
+    rt_scr[...] = jnp.zeros(rt_scr.shape, F32)
+    rt_scr[0:2, 0:tokens] = routes_ref[...].astype(F32)
+    columns_of = rt_scr[...].T[0:tokens].astype(jnp.int32)
     lane = iota((tokens, 128), 1)
-    first, second = routes_ref[:, 0:1], routes_ref[:, 1:2]
+    first, second = columns_of[:, 0:1], columns_of[:, 1:2]
     hits = jnp.where((first == lane) | (second == lane), 1.0, 0.0)
     below = jnp.where(iota((tokens, tokens), 1) < iota((tokens, tokens), 0), 1.0, 0.0).astype(BF16)
     ranks = mm(below, hits.astype(BF16))
     my_hit = jnp.sum(jnp.where(lane == ve, hits, 0.0), axis=1, keepdims=True)
     my_rank = jnp.sum(jnp.where(lane == ve, ranks, 0.0), axis=1, keepdims=True)
     mine = jnp.where((my_hit > 0.5) & (my_rank == lane.astype(F32)), 1.0, 0.0)
-    mine_half = mine.astype(BF16)
-
-    picked = mm_tn(mine_half, normed_ref[...])
-    ysend[...] = picked[0:slots].astype(BF16)
-    pl.semaphore_wait(barrier, 3 + vs - 1)
-    y_out = pltpu.make_async_remote_copy(
-        src_ref=ysend, dst_ref=yrecv, send_sem=y_sem.at[0], recv_sem=y_sem.at[1],
-        device_id={"fsdp": across}, device_id_type=MESH)
-    y_out.start()
-
-    logits = mm(normed_ref[...], router_ref[...])
+
+    picked = mm_tn(mine.astype(BF16), normed_ref[...])[0:block]
+    xbuf[0] = jnp.concatenate([picked[:, 0:cut], picked[:, cut:width]], axis=0).astype(BF16)
+    pl.semaphore_wait(barrier, 4 + vs - 1)
+
+    ways = (right, left)
+    steps = zs // 2
+    middle = (cut // 128 + 1) // 2 * 128
+    spans = (pl.ds(0, middle), pl.ds(middle, cut - middle))
+
+    def halves(step, way):
+        return (way,) if step == steps - 1 else (0, 1)
+
+    def gather_copy(way, step, h):
+        src = 0 if step == 0 else 2 * step - 1 + way
+        dst = zs - 1 if step == steps - 1 else 2 * step + 1 + way
+        return pltpu.make_async_remote_copy(
+            src_ref=xbuf.at[src, :, spans[h]], dst_ref=xbuf.at[dst, :, spans[h]],
+            send_sem=ag_sem.at[0, way, step, h], recv_sem=ag_sem.at[1, way, step, h],
+            device_id={"fsdp": ways[way]}, device_id_type=MESH)
+
+    def gather_step(step):
+        for h in (0, 1):
+            for way in range(2):
+                if step > 0:
+                    gather_copy(way, step - 1, h).wait_recv()
+                if h in halves(step, way):
+                    gather_copy(way, step, h).start()
+
+    def expert_up(first_block, count):
+        blocks = range(first_block, first_block + count)
+        sides = [
+            jnp.concatenate([xbuf[b, at : at + block, :].astype(F32) for b in blocks], axis=0)
+            for at in (0, block)
+        ]
+        rows = jnp.concatenate(sides, axis=1).astype(BF16)
+        gate = mm_nt(rows, weights[0:sources].reshape(sources * pitch, width))
+        lifted = mm_nt(rows, weights[sources : 2 * sources].reshape(sources * pitch, width))
+        return (gate / (1.0 + jnp.exp(-gate)) * lifted).astype(BF16)
+
+    def expert_down(acts, first_block, count):
+        tile = cut // 3
+        for side in range(2):
+            for c in range(3):
+                down = weights[2 * sources : 3 * sources, :, side * cut + c * tile : side * cut + (c + 1) * tile]
+                out = mm(acts, down.reshape(sources * pitch, tile))
+                for i in range(count):
+                    obuf[first_block + i, side * block : (side + 1) * block, c * tile : (c + 1) * tile] = (
+                        out[i * block : (i + 1) * block])
+
+    def down_copy(src, j, to):
+        return pltpu.make_async_remote_copy(
+            src_ref=src, dst_ref=wraw.at[2 * sources + j], send_sem=d_sem.at[0, j], recv_sem=d_sem.at[1, j],
+            device_id={"fsdp": to}, device_id_type=MESH)
+
+    down_far = down_copy(wd_ref, 2, across)
+    down_near = down_copy(wd_ref, 1, twin)
+    down_pass = down_copy(wraw.at[2 * sources + 2], 3, twin)
+    gather_step(0)
+    down_far.start()
+    down_near.start()
+    logits = mm_nt(normed_ref[...], router_ref[...])
     lane8 = iota(logits.shape, 1)
     chosen0 = jnp.sum(jnp.where(lane8 == first, logits, 0.0), axis=1, keepdims=True)
     chosen1 = jnp.sum(jnp.where(lane8 == second, logits, 0.0), axis=1, keepdims=True)
     gate0 = 1.0 / (1.0 + jnp.exp(chosen1 - chosen0))
     gate1 = 1.0 / (1.0 + jnp.exp(chosen0 - chosen1))
     my_gate = jnp.where(first == ve, gate0, jnp.where(second == ve, gate1, 0.0))
-    slot_gate = jnp.sum((mine * my_gate).T, axis=1, keepdims=True)[0:slots]
+    slot_gate = jnp.sum((mine * my_gate).T, axis=1, keepdims=True)[0:block]
     spread_e = jnp.where(iota((128, vs * slots), 0) == iota((128, vs * slots), 1) // slots, 1.0, 0.0).astype(BF16)
     all_hits = mm(hits.astype(BF16), spread_e)
     all_ranks = mm(ranks.astype(BF16), spread_e)
     slot_at = (iota((tokens, vs * slots), 1) % slots).astype(F32)
     back = jnp.where((all_hits > 0.5) & (all_ranks == slot_at), 1.0, 0.0).astype(BF16)
 
-    y_out.wait_recv()
-    xbuf[0] = jnp.concatenate([picked[0:block], yrecv[...].astype(F32)[0:block]], axis=0).astype(BF16)
-
-    cut = width // 2
-    ways = (right, left)
-    steps = zs // 2
-
-    def halves(step, way):
-        return (way,) if step == steps - 1 else (0, 1)
-
-    def gather_copy(way, step, h):
-        src = 0 if step == 0 else 2 * step - 1 + way
-        dst = zs - 1 if step == steps - 1 else 2 * step + 1 + way
-        at = pl.ds(h * cut, cut)
-        return pltpu.make_async_remote_copy(
-            src_ref=xbuf.at[src, :, at], dst_ref=xbuf.at[dst, :, at],
-            send_sem=ag_sem.at[0, way, step, h], recv_sem=ag_sem.at[1, way, step, h],
-            device_id={"fsdp": ways[way]}, device_id_type=MESH)
-
-    def expert(first_block, count):
-        rows = xbuf[first_block : first_block + count].reshape(count * pair, width)
-        acts = []
-        for j in range(2):
-            gate = mm(rows, wg[j])
-            acts.append((gate / (1.0 + jnp.exp(-gate)) * mm(rows, wu[j])).astype(BF16))
-        tile = width // 3
-        for c in range(3):
-            at = pl.ds(c * tile, tile)
-            out = mm(acts[0], wd[0, :, at]) + mm(acts[1], wd[1, :, at])
-            obuf[first_block : first_block + count, :, at] = out.reshape(count, pair, tile)
-
-    for step in range(steps):
-        for way in range(2):
-            for h in (0, 1):
-                if step > 0:
-                    gather_copy(way, step - 1, h).wait_recv()
-                if h in halves(step, way):
-                    gather_copy(way, step, h).start()
-        if step == 0:
-            for load in loads:
-                load.wait()
-            expert(0, 1)
-        else:
-            expert(2 * step - 1, 2)
+    for load in loads:
+        load.wait()
+
+    def settle(i, carry):
+        weights[i, pitch - 16 : pitch, :] = jnp.zeros((16, width), BF16)
+        weights[i, 0:hidden, :] = wraw[i]
+        return carry
+
+    lax.fori_loop(0, 2 * sources, settle, 0)
+    for step in range(1, steps):
+        gather_step(step)
+        if step == 2:
+            near_acts = expert_up(0, 5)
     for way in range(2):
         gather_copy(way, steps - 1, way).wait_recv()
-    expert(zs - 1, 1)
+    far_acts = expert_up(5, 3)
+    down_far.wait_recv()
+    down_pass.start()
+    down_near.wait_recv()
+    down_pass.wait_recv()
+    lax.fori_loop(2 * sources, 3 * sources, settle, 0)
+    expert_down(far_acts, 5, 3)
 
     def sum_copy(way, step, h):
-        at = pl.ds(h * cut, cut)
-        return pltpu.make_async_remote_copy(
-            src_ref=sbuf.at[way, step, :, at], dst_ref=rbuf.at[way, step, :, at],
+        return pltpu.make_async_remote_copy(
+            src_ref=sbuf.at[way, step, :, spans[h]], dst_ref=rbuf.at[way, step, :, spans[h]],
             send_sem=rs_sem.at[0, way, step, h], recv_sem=rs_sem.at[1, way, step, h],
             device_id={"fsdp": ways[way]}, device_id_type=MESH)
 
     for step in range(steps):
         for h in (0, 1):
+            at = spans[h]
             for way in range(2):
-                at = pl.ds(h * cut, cut)
                 if step == 0:
                     if h != way:
                         continue
@@ -537,21 +590,17 @@
                         value = value + rbuf[way, step - 1, :, at].astype(F32)
                     sbuf[way, step, :, at] = value.astype(BF16)
                 sum_copy(way, step, h).start()
+        if step == 0:
+            expert_down(near_acts, 0, 5)
     for way in range(2):
         for h in (0, 1):
             sum_copy(way, steps - 1, h).wait_recv()
     whole = obuf[0] + rbuf[0, steps - 1].astype(F32) + rbuf[1, steps - 1].astype(F32)
-    yback[...] = jnp.concatenate(
-        [whole[block:pair], jnp.zeros((slots - block, width), F32)], axis=0).astype(BF16)
-    b_out = pltpu.make_async_remote_copy(
-        src_ref=yback, dst_ref=yhome, send_sem=b_sem.at[0], recv_sem=b_sem.at[1],
-        device_id={"fsdp": across}, device_id_type=MESH)
-    b_out.start()
-    b_out.wait_recv()
-    gated = (whole[0:slots] + yhome[...].astype(F32)) * slot_gate
+    gated = [whole[side * block : (side + 1) * block] * slot_gate for side in range(2)]
 
     columns = width // vs
     padded = fsend.shape[2]
+    empty = jnp.zeros((slots - block, padded), F32)
 
     def f_copy(k, to, slot):
         return pltpu.make_async_remote_copy(
@@ -559,8 +608,9 @@
             device_id={"vocab": to}, device_id_type=MESH)
 
     for v in range(vs):
-        turned = gated if v == 0 else pltpu.roll(gated, width - v * columns, 1)
-        fsend[v] = turned[:, 0:padded].astype(BF16)
+        side, at = divmod(v * columns, cut)
+        turned = gated[side] if at == 0 else pltpu.roll(gated[side], cut - at, 1)
+        fsend[v] = jnp.concatenate([turned[:, 0:padded], empty], axis=0).astype(BF16)
     for k in range(1, vs):
         f_copy(k, lax.rem(ve + k, vs), ve).start()
     frecv[ve] = fsend[ve]
@@ -569,8 +619,8 @@
     mixture = mm(back, frecv[...].reshape(vs * slots, padded))
     out_ref[...] = (cols_ref[...] + mixture)[:, 0:columns].astype(BF16)
 
-    y_out.wait_send()
-    b_out.wait_send()
+    for copy in (down_far, down_near, down_pass):
+        copy.wait_send()
     for step in range(steps):
         for way in range(2):
             for h in halves(step, way):
@@ -595,6 +645,7 @@
     tree = parents.shape[1]
     pool_pages, page_rows, _ = pool_keys.shape
     hidden = gate_weight.shape[2]
+    pitch = -(-hidden // 64) * 64
     vmem = pl.BlockSpec(memory_space=pltpu.VMEM)
     smem = pl.BlockSpec(memory_space=pltpu.SMEM)
     hbm = pl.BlockSpec(memory_space=pl.ANY)
@@ -602,16 +653,15 @@
     padded = -(-(width // vs) // 128) * 128
     per_owner = 16
     owners = tokens // per_owner
-    wg, wu, wd = gate_weight[0], up_weight[0], down_weight[0]
-    like = lambda a: jax.ShapeDtypeStruct(a.shape, a.dtype)
-    normed, cols, wg2, wu2, wd2 = pl.pallas_call(
+    wg, wu, wd = gate_weight[0].T, up_weight[0].T, down_weight[0]
+    normed, cols, more = pl.pallas_call(
         functools.partial(attention_kernel, fs, vs),
         out_shape=(
             jax.ShapeDtypeStruct((owners, per_owner, width), BF16),
             jax.ShapeDtypeStruct((owners, per_owner, padded), F32),
-            like(wg), like(wu), like(wd)),
-        in_specs=[vmem] * 4 + [smem] * 2 + [vmem] * 4 + [hbm] * 5,
-        out_specs=(vmem, vmem, hbm, hbm, hbm),
+            jax.ShapeDtypeStruct((6, hidden, width), BF16)),
+        in_specs=[vmem] * 4 + [smem] * 2 + [vmem] * 4 + [hbm] * 4,
+        out_specs=(vmem, vmem, hbm),
         scratch_shapes=[
             pltpu.VMEM(pool_keys.shape, BF16),
             pltpu.VMEM(pool_values.shape, BF16),
@@ -621,17 +671,17 @@
             pltpu.VMEM((256, 128), F32),
             pltpu.VMEM((fs, tree, features), BF16),
             pltpu.VMEM((fs, tree, features), BF16),
-            pltpu.VMEM((fs, 8, 128), F32),
-            pltpu.VMEM((fs, 8, 128), F32),
+            pltpu.VMEM((fs, 1, 128), F32),
+            pltpu.VMEM((fs, 1, 128), F32),
             pltpu.VMEM((fs, tree, features), BF16),
             pltpu.VMEM((fs, tree, features), BF16),
-            pltpu.VMEM((fs, 8, 128), F32),
-            pltpu.VMEM((fs, 8, 128), F32),
+            pltpu.VMEM((fs, 4, 128), F32),
+            pltpu.VMEM((fs, 4, 128), F32),
             pltpu.VMEM((owners, per_owner, width), F32),
             pltpu.VMEM((owners, per_owner, width), BF16),
             pltpu.VMEM((vs, per_owner, width), BF16),
             pltpu.VMEM((vs, per_owner, padded), F32),
-            dma((4,)), dma((2, 3)), dma((2, fs)), dma((2, fs)), dma((2, fs)), dma((2, fs)),
+            dma((4,)), dma((2, 6)), dma((2, fs)), dma((2, fs)), dma((2, fs)), dma((2, fs)),
             dma((2, vs)), dma((2, vs)), dma((2, vs)),
         ],
         compiler_params=pltpu.CompilerParams(
@@ -639,34 +689,30 @@
         name="attention",
     )(
         queries, new_keys, new_values, page_table, cache_lengths, serve_pages.reshape(-1), parents,
-        resid.reshape(owners, per_owner, width), out_weight, norm_gain.reshape(1, width),
-        pool_keys, pool_values, wg, wu, wd)
-    pair, slots = 80, 48
+        resid.reshape(owners, per_owner, width), out_weight, norm_gain,
+        pool_keys, pool_values, wg, wu)
+    block, slots = 40, 48
     return pl.pallas_call(
         functools.partial(expert_kernel, fs, vs, zs),
         out_shape=jax.ShapeDtypeStruct((tokens, width // vs), BF16),
-        in_specs=[vmem] * 4 + [hbm] * 6,
+        in_specs=[vmem] * 4 + [hbm] * 4,
         out_specs=vmem,
         scratch_shapes=[
-            pltpu.VMEM((2, width, hidden), BF16),
-            pltpu.VMEM((2, width, hidden), BF16),
-            pltpu.VMEM((2, hidden, width), BF16),
-            pltpu.VMEM((zs, pair, width), BF16),
-            pltpu.VMEM((zs, pair, width), F32),
-            pltpu.VMEM((2, zs // 2, pair, width), BF16),
-            pltpu.VMEM((2, zs // 2, pair, width), BF16),
-            pltpu.VMEM((slots, width), BF16),
-            pltpu.VMEM((slots, width), BF16),
-            pltpu.VMEM((slots, width), BF16),
-            pltpu.VMEM((slots, width), BF16),
+            pltpu.VMEM((12, hidden, width), BF16),
+            pltpu.VMEM((12, pitch, width), BF16),
+            pltpu.VMEM((128, 128), F32),
+            pltpu.VMEM((zs, 2 * block, width // 2), BF16),
+            pltpu.VMEM((zs, 2 * block, width // 2), F32),
+            pltpu.VMEM((2, zs // 2, 2 * block, width // 2), BF16),
+            pltpu.VMEM((2, zs // 2, 2 * block, width // 2), BF16),
             pltpu.VMEM((vs, slots, padded), BF16),
             pltpu.VMEM((vs, slots, padded), BF16),
-            dma((6,)), dma((2, 2, zs // 2, 2)), dma((2, 2, zs // 2, 2)), dma((2,)), dma((2,)), dma((2, vs)),
+            dma((12,)), dma((2, 4)), dma((2, 2, zs // 2, 2)), dma((2, 2, zs // 2, 2)), dma((2, vs)),
         ],
         compiler_params=pltpu.CompilerParams(
             collective_id=2, has_side_effects=True, vmem_limit_bytes=56 * 2**20),
         name="experts",
-    )(normed.reshape(tokens, width), cols.reshape(tokens, padded), routes, router, wg, wu, wd, wg2, wu2, wd2)
+    )(normed.reshape(tokens, width), cols.reshape(tokens, padded), routes.T, router.T, wg, wu, wd, more)
 
 
 def solution(mesh):

time: 174 us -> 149 us (0.86)
  Pallas kernels: 164 us -> 147 us
  local copies, waits for them, and re-layouts: 9.86 us -> 1.52 us
    pallas_call x1, Pallas kernels: 87.2 us -> 54.9 us  [per_device(): pl.pallas_call(functools.partial(expert_kernel, fs, vs, zs), out_shape=ja...]
    pallas_call x1, Pallas kernels: 76.4 us -> 92.1 us  [per_device(): pl.pallas_call(functools.partial(attention_kernel, fs, vs), out_shape=(ja...]
    unnamed x7 -> x1, local copies, waits for them, and re-layouts: 8.55 us -> 1.52 us
where the time goes in v2:
time: 149 us
  Pallas kernels  147 us (99%)
  local copies, waits for them, and re-layouts  1.52 us (1%)
    pallas_call x1, Pallas kernels, per_device(): pl.pallas_call(functools.partial(attention_kernel, fs, vs), out_shape=(ja...  92.1 us
    pallas_call x1, Pallas kernels, per_device(): pl.pallas_call(functools.partial(expert_kernel, fs, vs, zs), out_shape=ja...  54.9 us

profile of v2, /device:TPU:32, one launch (start us, length us, event | category | flops | bytes accessed | tf_op | source)
XLA Modules:
  0.0 148.5 jit_solution(9740202101860861069)
XLA Ops:
  0.0 92.1 %attention.1 = (bf16[6,16,2304]{2,1,0:T(8,128)(2,1)}, f32[6,16,384]{2,1,0:T(8,128)}, bf16[6,180,2304]{2,1,0:T(8,128)(2,1)}) custom-call(bf16[96,256]{1,0:T(8,128)(2,1)} %q_ref.1, bf16[96,256]{1,0:T(8,128)(2,1)} %nk_ref.1, bf16[96,256]{1,0:T(8,128)(2,1)} %nv_ref.1, s32[2,32]{1,0:T(2,128)} %table_ref.1, s32[2]{0:T(128)} %length_ref.1, s32[32]{0:T(128)} %bitcast.23, ...), custom_call_target="tpu_custom_call" | custom-call | tf_op jit(solution)/shard_map/attention/pallas_call | solution.py:657
  92.1 54.9 %experts.1 = bf16[96,288]{1,0:T(8,128)(2,1)} custom-call(bf16[96,2304]{1,0:T(8,128)(2,1)} %bitcast.19, f32[96,384]{1,0:T(8,128)} %bitcast.20, s32[2,96]{1,0:T(2,128)} %bitcast.22, bf16[8,2304]{1,0:T(8,128)(2,1)} %bitcast.21, bf16[180,2304]{1,0:T(8,128)(2,1)} %bitcast.14, bf16[180,2304]{1,0:T(8,128)(2,1)} %bitcast.16, bf16[180,2304]{1,0:T(8,128)(2,1)} %bitcast.17, ...), custom_call_target="tpu_custom_call" | custom-call | tf_op jit(solution)/shard_map/experts/pallas_call | solution.py:695
  147.0 1.5 %copy.19 = bf16[96,288]{1,0:T(8,128)(2,1)} copy(bf16[96,288]{1,0:T(8,128)(2,1)} %experts.1) | data formatting | bytes 110592

commit v3 on v2

--- a/solution.py
+++ b/solution.py
@@ -33,13 +33,13 @@
 
 
 def attention_kernel(
-    fs, vs,
+    fs, vs, zs,
     q_ref, nk_ref, nv_ref, table_ref, length_ref, serve_ref, parent_ref, resid_ref, ow_ref, gain_ref,
     pk_ref, pv_ref, wg_ref, wu_ref,
     normed_ref, cols_ref, more_ref,
-    kbuf, vbuf, s_scr, lim_scr, rq_scr, wt_scr, qsend, qrecv, msend, mrecv, osend, orecv, tsend, trecv,
+    kbuf, vbuf, s_scr, lim_scr, rq_scr, wt_scr, qall, msend, mrecv, osend, orecv, tsend, trecv,
     pown, psend, precv, hsend,
-    local_sem, w_sem, q_sem, m_sem, o_sem, t_sem, p_sem, n_sem, h_sem,
+    local_sem, w_sem, q_sem, y_sem, r_sem, c_sem, m_sem, o_sem, t_sem, p_sem, n_sem, h_sem,
 ):
     requests, pages_each = table_ref.shape
     tree = parent_ref.shape[1]
@@ -56,6 +56,22 @@
     ve = lax.axis_index("vocab")
     twin = me + 1 - 2 * lax.rem(me, 2)
     across = lax.rem(me + fs // 2, fs)
+    core = lax.rem(me, 2)
+    z = lax.rem(me // 2, zs)
+    yhi = me // (2 * zs)
+    right = (yhi * zs + lax.rem(z + 1, zs)) * 2 + core
+    left = (yhi * zs + lax.rem(z + zs - 1, zs)) * 2 + core
+
+    def device_at(slot):
+        step = slot // 4
+        odd = step % 2
+        dz = (step // 2) * (1 - odd) - ((step + 1) // 2) * odd
+        return (((yhi + (slot // 2) % 2) % 2) * zs + (z + dz + zs) % zs) * 2 + (core + slot % 2) % 2
+
+    def mirrored(slot):
+        step = slot // 4
+        turned = jnp.minimum(jnp.maximum(step - 1 + 2 * (step % 2), 0), zs - 1)
+        return 4 * turned + slot % 4
 
     barrier = pltpu.get_barrier_semaphore()
 
@@ -73,7 +89,7 @@
     pool_copies = [
         pltpu.make_async_copy(src.at[pl.ds(at, half)], dst.at[pl.ds(at, half)], local_sem.at[i])
         for i, (src, dst, at) in enumerate(
-            ((pk_ref, kbuf, 0), (pv_ref, vbuf, 0), (pk_ref, kbuf, half), (pv_ref, vbuf, half))
+            ((pk_ref, kbuf, half), (pv_ref, vbuf, half), (pk_ref, kbuf, 0), (pv_ref, vbuf, 0))
         )
     ]
     for copy in pool_copies:
@@ -91,50 +107,68 @@
     (seen0, seen1), _ = lookup(sub)
     lane_w = iota((local_pages, 2 * wide), 1)
     lim_scr[...] = jnp.where(lane_w < wide, seen0, seen1).astype(jnp.int32)
-    holder = lax.rem(sub + me, fs)
-    (far0, far1), far_rq = lookup(holder + pool_pages)
+    (far0, far1), far_rq = lookup(device_at(sub) + pool_pages)
     rq_scr[...] = jnp.broadcast_to(far_rq, rq_scr.shape)
-    msend[...] = jnp.broadcast_to((far0 + far1)[:, :, None], msend.shape)
+    msend[...] = jnp.where(iota(msend.shape, 1) == 0, (far0 + far1)[:, :, None], far_rq[:, :, None])
+    qall[0] = q_ref[...]
 
     pl.semaphore_wait(barrier, fs - 1 + vs - 1)
 
-    q0 = q_ref[0:tree, :].astype(F32)
-    q1 = q_ref[tree : 2 * tree, :].astype(F32)
-
-    def q_copy(k, to):
-        return pltpu.make_async_remote_copy(
-            src_ref=qsend.at[k], dst_ref=qrecv.at[k], send_sem=q_sem.at[0, k], recv_sem=q_sem.at[1, k],
+    def q_copy(src, dst, send_sem, to):
+        return pltpu.make_async_remote_copy(
+            src_ref=qall.at[src], dst_ref=qall.at[dst], send_sem=send_sem, recv_sem=q_sem.at[dst],
             device_id={"fsdp": to}, device_id_type=MESH)
 
-    def m_copy(k, to):
-        return pltpu.make_async_remote_copy(
-            src_ref=msend.at[k], dst_ref=mrecv.at[k], send_sem=m_sem.at[0, k], recv_sem=m_sem.at[1, k],
+    y_copy = q_copy(0, 2, y_sem.at[0], across)
+    last = zs // 2 - 1
+
+    def ring_copy(way, step, dy):
+        src = 0 if step == 0 else 2 * step - 1 + way
+        dst = zs - 1 if step == last else 2 * step + 1 + way
+        return q_copy(4 * src + 2 * dy, 4 * dst + 2 * dy, r_sem.at[way, step, dy], (right, left)[way])
+
+    def twin_copy(slot):
+        return q_copy(slot, slot + 1, c_sem.at[slot // 2], twin)
+
+    def arrived(slot):
+        q_copy(slot, slot, y_sem.at[0], me).wait_recv()
+
+    def ring_step(step, dy):
+        for way in range(2):
+            if step > 0:
+                arrived(4 * (2 * step - 1 + way) + 2 * dy)
+            if step < last or way == dy:
+                ring_copy(way, step, dy).start()
+            if step > 0:
+                twin_copy(4 * (2 * step - 1 + way) + 2 * dy).start()
+
+    def parts_copy(send, recv, sem, src, dst, to):
+        return pltpu.make_async_remote_copy(
+            src_ref=send.at[src], dst_ref=recv.at[dst], send_sem=sem.at[0, src], recv_sem=sem.at[1, dst],
             device_id={"fsdp": to}, device_id_type=MESH)
 
-    def o_copy(k, to):
-        return pltpu.make_async_remote_copy(
-            src_ref=osend.at[k], dst_ref=orecv.at[k], send_sem=o_sem.at[0, k], recv_sem=o_sem.at[1, k],
-            device_id={"fsdp": to}, device_id_type=MESH)
-
-    def t_copy(k, to):
-        return pltpu.make_async_remote_copy(
-            src_ref=tsend.at[k], dst_ref=trecv.at[k], send_sem=t_sem.at[0, k], recv_sem=t_sem.at[1, k],
-            device_id={"fsdp": to}, device_id_type=MESH)
-
-    def pick_query(k):
-        pick = rq_scr[pl.ds(k, 1), :]
-        return (q0 * (1.0 - pick) + q1 * pick).astype(BF16)
-
-    def send_query(k, carry):
-        qsend[k] = pick_query(k)
-        to = lax.rem(me + k, fs)
-        q_copy(k, to).start()
-        m_copy(k, to).start()
+    def m_copy(src, dst, to):
+        return parts_copy(msend, mrecv, m_sem, src, dst, to)
+
+    def o_copy(src, dst, to):
+        return parts_copy(osend, orecv, o_sem, src, dst, to)
+
+    def t_copy(src, dst, to):
+        return parts_copy(tsend, trecv, t_sem, src, dst, to)
+
+    y_copy.start()
+    ring_step(0, 0)
+    twin_copy(0).start()
+
+    def send_limits(k, carry):
+        m_copy(k, mirrored(k), device_at(k)).start()
         return carry
 
-    lax.fori_loop(1, fs, send_query, 0)
-    qrecv[0] = pick_query(0)
+    lax.fori_loop(1, fs, send_limits, 0)
     mrecv[0] = msend[0]
+    arrived(2)
+    ring_step(0, 1)
+    twin_copy(2).start()
 
     kinds = (wg_ref, wu_ref)
 
@@ -145,8 +179,7 @@
 
     far_copies = [weight_copy(src, 2 + i, across) for i, src in enumerate(kinds)]
     near_copies = [weight_copy(src, i, twin) for i, src in enumerate(kinds)]
-    pass_copies = [weight_copy(more_ref.at[2 + i], 4 + i, twin) for i in range(2)]
-    for copy in far_copies + near_copies:
+    for copy in far_copies[:1] + near_copies:
         copy.start()
 
     head_of = iota((1, features), 1) // HEAD_DIM
@@ -165,6 +198,63 @@
 
     spread_q = [spread(q_ref[r * tree : (r + 1) * tree, :]) for r in range(requests)]
     both_q = jnp.concatenate(spread_q, axis=0)
+
+    for copy in pool_copies:
+        copy.wait()
+    stat_row = iota((4, 128), 0)
+    held_row = iota((page_rows, wide), 0)
+
+    def serve_one(k):
+        page = serve_ref[device_at(k)]
+        told = mrecv[k]
+        told = jnp.concatenate([told, told], axis=1)
+        limit, pick = told[0:1], told[1:2]
+        asked = qall[k].astype(F32)
+        query = (asked[0:tree] * (1.0 - pick) + asked[tree : 2 * tree] * pick).astype(BF16)
+        scores = mm_nt(kbuf[page], spread(query))
+        scores = jnp.where(held_row < limit.astype(jnp.int32), scores, NEGATIVE)
+        best = jnp.max(scores, axis=0, keepdims=True)
+        weights = jnp.exp(scores - best).astype(BF16)
+        amount = jnp.sum(weights.astype(F32), axis=0, keepdims=True)
+        osend[k] = gather_heads(mm_tn(weights, vbuf[page])).astype(BF16)
+        tsend[k] = jnp.where(
+            stat_row == 0, best[:, 0:128],
+            jnp.where(stat_row == 1, best[:, 128:256],
+                      jnp.where(stat_row == 2, amount[:, 0:128], amount[:, 128:256])))
+
+    group = 4
+
+    def serve_step(step, carry):
+        for i in range(group):
+            k = step * group + i
+
+            @pl.when(k > 0)
+            def _():
+                m_copy(k, k, me).wait_recv()
+
+            if i % 2 == 1:
+                arrived(k)
+        for i in range(group):
+            serve_one(step * group + i)
+        for i in range(group):
+            k = step * group + i
+
+            @pl.when(k > 0)
+            def _():
+                o_copy(k, mirrored(k), device_at(k)).start()
+                t_copy(k, mirrored(k), device_at(k)).start()
+
+        return carry
+
+    for step in range(1, last + 1):
+        for dy in range(2):
+            ring_step(step, dy)
+        lax.fori_loop(max(0, 2 * step - 3), 2 * step - 1, serve_step, 0)
+    for dy in range(2):
+        arrived(4 * (zs - 1) + 2 * dy)
+        twin_copy(4 * (zs - 1) + 2 * dy).start()
+    lax.fori_loop(2 * last - 1, zs, serve_step, 0)
+    far_copies[1].start()
 
     eye = jnp.where(iota((tree, tree), 0) == iota((tree, tree), 1), 1.0, 0.0)
     tile_heads = jnp.where(
@@ -182,7 +272,6 @@
         tree_scores.append(jnp.where(seen > 0.5, scores, NEGATIVE))
     top = jnp.concatenate([jnp.max(s, axis=0, keepdims=True) for s in tree_scores], axis=1)
 
-    pool_copies[0].wait()
     key_row = iota((page_rows, 2 * wide), 0)
     chunk = 4
 
@@ -195,8 +284,8 @@
             top = jnp.maximum(top, jnp.max(scores, axis=0, keepdims=True))
         return top
 
-    top = lax.fori_loop(0, local_pages // chunk, score_chunk, top)
-    pool_copies[1].wait()
+    chunks = local_pages // chunk
+    top = lax.fori_loop(0, chunks, score_chunk, top)
 
     def mix_chunk(c, carry):
         total, mixed = carry
@@ -207,7 +296,7 @@
         return total, mixed + mm_tn(weights, values)
 
     total, mixed = lax.fori_loop(
-        0, local_pages // chunk, mix_chunk,
+        0, chunks, mix_chunk,
         (jnp.zeros((1, 2 * wide), F32), jnp.zeros((2 * wide, features), F32)))
     own_top, own_total, own_mix = [], [], []
     for r in range(requests):
@@ -219,60 +308,11 @@
         mix_r = mixed[r * wide : (r + 1) * wide] + mm_tn(weights, nv_ref[r * tree : (r + 1) * tree, :])
         own_mix.append(gather_heads(mix_r))
 
-    pool_copies[2].wait()
-    pool_copies[3].wait()
-    stat_row = iota((4, 128), 0)
-    held_row = iota((page_rows, wide), 0)
-
-    def serve_one(k):
-        asker = lax.rem(me - k + fs, fs)
-        page = serve_ref[asker]
-        limit = mrecv[k]
-        limit = jnp.concatenate([limit, limit], axis=1)
-        scores = mm_nt(kbuf[page], spread(qrecv[k]))
-        scores = jnp.where(held_row < limit.astype(jnp.int32), scores, NEGATIVE)
-        best = jnp.max(scores, axis=0, keepdims=True)
-        weights = jnp.exp(scores - best).astype(BF16)
-        amount = jnp.sum(weights.astype(F32), axis=0, keepdims=True)
-        osend[k] = gather_heads(mm_tn(weights, vbuf[page])).astype(BF16)
-        tsend[k] = jnp.where(
-            stat_row == 0, best[:, 0:128],
-            jnp.where(stat_row == 1, best[:, 128:256],
-                      jnp.where(stat_row == 2, amount[:, 0:128], amount[:, 128:256])))
-
-    group = 4
-
-    def serve_group(first):
-        base = first * group
-        for i in range(group):
-            k = base + i
-
-            @pl.when(k > 0)
-            def _():
-                q_copy(k, me).wait_recv()
-                m_copy(k, me).wait_recv()
-
-        for i in range(group):
-            serve_one(base + i)
-        for i in range(group):
-            k = base + i
-
-            @pl.when(k > 0)
-            def _():
-                to = lax.rem(me - k + fs, fs)
-                o_copy(k, to).start()
-                t_copy(k, to).start()
-
-    def serve_step(first, carry):
-        serve_group(first)
-        return carry
-
-    lax.fori_loop(0, fs // group, serve_step, 0)
     orecv[0] = osend[0]
     trecv[0] = tsend[0]
 
     def await_stats(k, carry):
-        t_copy(k, me).wait_recv()
+        t_copy(k, k, me).wait_recv()
         return carry
 
     lax.fori_loop(1, fs, await_stats, 0)
@@ -309,7 +349,7 @@
         return out
 
     def await_parts(k, carry):
-        o_copy(k, me).wait_recv()
+        o_copy(k, k, me).wait_recv()
         return carry
 
     lax.fori_loop(1, fs, await_parts, 0)
@@ -361,10 +401,6 @@
         @pl.when(owns(to))
         def _():
             p_copy(k, to).start()
-
-    for far, onward in zip(far_copies, pass_copies):
-        far.wait_recv()
-        onward.start()
 
     @pl.when(owns(ve))
     def _():
@@ -394,13 +430,21 @@
             h_copy(k, share(owner), ve).wait_recv()
 
     def await_sends(k, carry):
-        q_copy(k, me).wait_send()
-        m_copy(k, me).wait_send()
-        o_copy(k, me).wait_send()
-        t_copy(k, me).wait_send()
+        m_copy(k, k, me).wait_send()
+        o_copy(k, k, me).wait_send()
+        t_copy(k, k, me).wait_send()
         return carry
 
     lax.fori_loop(1, fs, await_sends, 0)
+    y_copy.wait_send()
+    for step in range(zs):
+        for dy in range(2):
+            twin_copy(4 * step + 2 * dy).wait_send()
+    for step in range(last + 1):
+        for way in range(2):
+            for dy in range(2):
+                if step < last or way == dy:
+                    ring_copy(way, step, dy).wait_send()
     for k in range(1, vs):
         to = lax.rem(ve + k, vs)
 
@@ -415,9 +459,7 @@
             n_copy(k, own, to).wait_send()
             h_copy(k, own, to).wait_send()
 
-    for copy in far_copies:
-        copy.wait_send()
-    for copy in near_copies + pass_copies:
+    for copy in far_copies + near_copies:
         copy.wait()
 
 
@@ -426,7 +468,7 @@
     normed_ref, cols_ref, routes_ref, router_ref, wg_ref, wu_ref, wd_ref, more_ref,
     out_ref,
     wraw, weights, rt_scr, xbuf, obuf, sbuf, rbuf, fsend, frecv,
-    w_sem, d_sem, ag_sem, rs_sem, f_sem,
+    w_sem, d_sem, p_sem, ag_sem, rs_sem, f_sem,
 ):
     tokens, width = normed_ref.shape
     block = xbuf.shape[1] // 2
@@ -453,7 +495,7 @@
     loads = []
     for i, src in enumerate((wg_ref, wu_ref, wd_ref)):
         loads.append(pltpu.make_async_copy(src, wraw.at[i * sources], w_sem.at[i * sources]))
-        for j in range(1, sources if i < 2 else 1):
+        for j in range(1, sources - 1 if i < 2 else 1):
             loads.append(pltpu.make_async_copy(
                 more_ref.at[(j - 1) * 2 + i], wraw.at[i * sources + j], w_sem.at[i * sources + j]))
     for load in loads:
@@ -528,7 +570,15 @@
     down_far = down_copy(wd_ref, 2, across)
     down_near = down_copy(wd_ref, 1, twin)
     down_pass = down_copy(wraw.at[2 * sources + 2], 3, twin)
+    up_pass = [
+        pltpu.make_async_remote_copy(
+            src_ref=more_ref.at[2 + i], dst_ref=wraw.at[i * sources + 3],
+            send_sem=p_sem.at[0, i], recv_sem=p_sem.at[1, i], device_id={"fsdp": twin}, device_id_type=MESH)
+        for i in range(2)
+    ]
     gather_step(0)
+    for copy in up_pass:
+        copy.start()
     down_far.start()
     down_near.start()
     logits = mm_nt(normed_ref[...], router_ref[...])
@@ -547,6 +597,8 @@
 
     for load in loads:
         load.wait()
+    for copy in up_pass:
+        copy.wait_recv()
 
     def settle(i, carry):
         weights[i, pitch - 16 : pitch, :] = jnp.zeros((16, width), BF16)
@@ -619,7 +671,7 @@
     mixture = mm(back, frecv[...].reshape(vs * slots, padded))
     out_ref[...] = (cols_ref[...] + mixture)[:, 0:columns].astype(BF16)
 
-    for copy in (down_far, down_near, down_pass):
+    for copy in (down_far, down_near, down_pass, *up_pass):
         copy.wait_send()
     for step in range(steps):
         for way in range(2):
@@ -655,11 +707,11 @@
     owners = tokens // per_owner
     wg, wu, wd = gate_weight[0].T, up_weight[0].T, down_weight[0]
     normed, cols, more = pl.pallas_call(
-        functools.partial(attention_kernel, fs, vs),
+        functools.partial(attention_kernel, fs, vs, zs),
         out_shape=(
             jax.ShapeDtypeStruct((owners, per_owner, width), BF16),
             jax.ShapeDtypeStruct((owners, per_owner, padded), F32),
-            jax.ShapeDtypeStruct((6, hidden, width), BF16)),
+            jax.ShapeDtypeStruct((4, hidden, width), BF16)),
         in_specs=[vmem] * 4 + [smem] * 2 + [vmem] * 4 + [hbm] * 4,
         out_specs=(vmem, vmem, hbm),
         scratch_shapes=[
@@ -669,10 +721,9 @@
             pltpu.VMEM((pool_pages // 2, 512), jnp.int32),
             pltpu.VMEM((fs, features), F32),
             pltpu.VMEM((256, 128), F32),
-            pltpu.VMEM((fs, tree, features), BF16),
-            pltpu.VMEM((fs, tree, features), BF16),
-            pltpu.VMEM((fs, 1, 128), F32),
-            pltpu.VMEM((fs, 1, 128), F32),
+            pltpu.VMEM((fs, 2 * tree, features), BF16),
+            pltpu.VMEM((fs, 2, 128), F32),
+            pltpu.VMEM((fs, 2, 128), F32),
             pltpu.VMEM((fs, tree, features), BF16),
             pltpu.VMEM((fs, tree, features), BF16),
             pltpu.VMEM((fs, 4, 128), F32),
@@ -681,7 +732,8 @@
             pltpu.VMEM((owners, per_owner, width), BF16),
             pltpu.VMEM((vs, per_owner, width), BF16),
             pltpu.VMEM((vs, per_owner, padded), F32),
-            dma((4,)), dma((2, 6)), dma((2, fs)), dma((2, fs)), dma((2, fs)), dma((2, fs)),
+            dma((4,)), dma((2, 4)), dma((fs,)), dma((1,)), dma((2, zs // 2, 2)), dma((fs // 2,)),
+            dma((2, fs)), dma((2, fs)), dma((2, fs)),
             dma((2, vs)), dma((2, vs)), dma((2, vs)),
         ],
         compiler_params=pltpu.CompilerParams(
@@ -707,7 +759,7 @@
             pltpu.VMEM((2, zs // 2, 2 * block, width // 2), BF16),
             pltpu.VMEM((vs, slots, padded), BF16),
             pltpu.VMEM((vs, slots, padded), BF16),
-            dma((12,)), dma((2, 4)), dma((2, 2, zs // 2, 2)), dma((2, 2, zs // 2, 2)), dma((2, vs)),
+            dma((12,)), dma((2, 4)), dma((2, 2)), dma((2, 2, zs // 2, 2)), dma((2, 2, zs // 2, 2)), dma((2, vs)),
         ],
         compiler_params=pltpu.CompilerParams(
             collective_id=2, has_side_effects=True, vmem_limit_bytes=56 * 2**20),

time: 149 us -> 138 us (0.926)
  Pallas kernels: 147 us -> 136 us
    pallas_call x1, Pallas kernels: 92.1 us -> 82.5 us  [per_device(): pl.pallas_call(functools.partial(attention_kernel, fs, vs, zs), out_shape...]
    pallas_call x1, Pallas kernels: 54.9 us -> 53.4 us  [per_device(): pl.pallas_call(functools.partial(expert_kernel, fs, vs, zs), out_shape=ja...]
where the time goes in v3:
time: 138 us; the launch traced here: 137 us
  Pallas kernels  136 us (99%)
  local copies, waits for them, and re-layouts  1.52 us (1%)
    pallas_call x1, Pallas kernels, per_device(): pl.pallas_call(functools.partial(attention_kernel, fs, vs, zs), out_shape...  82.5 us
    pallas_call x1, Pallas kernels, per_device(): pl.pallas_call(functools.partial(expert_kernel, fs, vs, zs), out_shape=ja...  53.4 us

profile of v3, /device:TPU:32, one launch (start us, length us, event | category | flops | bytes accessed | tf_op | source)
XLA Modules:
  0.0 137.4 jit_solution(2945658509294656857)
XLA Ops:
  0.0 82.5 %attention.1 = (bf16[6,16,2304]{2,1,0:T(8,128)(2,1)}, f32[6,16,384]{2,1,0:T(8,128)}, bf16[4,180,2304]{2,1,0:T(8,128)(2,1)}) custom-call(bf16[96,256]{1,0:T(8,128)(2,1)} %q_ref.1, bf16[96,256]{1,0:T(8,128)(2,1)} %nk_ref.1, bf16[96,256]{1,0:T(8,128)(2,1)} %nv_ref.1, s32[2,32]{1,0:T(2,128)} %table_ref.1, s32[2]{0:T(128)} %length_ref.1, s32[32]{0:T(128)} %bitcast.23, ...), custom_call_target="tpu_custom_call" | custom-call | tf_op jit(solution)/shard_map/attention/pallas_call | solution.py:709
  82.5 53.4 %experts.1 = bf16[96,288]{1,0:T(8,128)(2,1)} custom-call(bf16[96,2304]{1,0:T(8,128)(2,1)} %bitcast.19, f32[96,384]{1,0:T(8,128)} %bitcast.20, s32[2,96]{1,0:T(2,128)} %bitcast.22, bf16[8,2304]{1,0:T(8,128)(2,1)} %bitcast.21, bf16[180,2304]{1,0:T(8,128)(2,1)} %bitcast.14, bf16[180,2304]{1,0:T(8,128)(2,1)} %bitcast.16, bf16[180,2304]{1,0:T(8,128)(2,1)} %bitcast.17, ...), custom_call_target="tpu_custom_call" | custom-call | tf_op jit(solution)/shard_map/experts/pallas_call | solution.py:747
  135.9 1.5 %copy.19 = bf16[96,288]{1,0:T(8,128)(2,1)} copy(bf16[96,288]{1,0:T(8,128)(2,1)} %experts.1) | data formatting | bytes 110592

commit v4 on v3

--- a/solution.py
+++ b/solution.py
@@ -32,11 +32,11 @@
     return lax.broadcasted_iota(jnp.int32, shape, dim)
 
 
-def attention_kernel(
+def attention_part(
     fs, vs, zs,
     q_ref, nk_ref, nv_ref, table_ref, length_ref, serve_ref, parent_ref, resid_ref, ow_ref, gain_ref,
-    pk_ref, pv_ref, wg_ref, wu_ref,
-    normed_ref, cols_ref, more_ref,
+    pk_ref, pv_ref, wg_ref, wu_ref, wd_ref, wraw,
+    normed_ref, cols_ref,
     kbuf, vbuf, s_scr, lim_scr, rq_scr, wt_scr, qall, msend, mrecv, osend, orecv, tsend, trecv,
     pown, psend, precv, hsend,
     local_sem, w_sem, q_sem, y_sem, r_sem, c_sem, m_sem, o_sem, t_sem, p_sem, n_sem, h_sem,
@@ -170,16 +170,18 @@
     ring_step(0, 1)
     twin_copy(2).start()
 
-    kinds = (wg_ref, wu_ref)
+    kinds = (wg_ref, wu_ref, wd_ref)
 
     def weight_copy(src, at, to):
         return pltpu.make_async_remote_copy(
-            src_ref=src, dst_ref=more_ref.at[at], send_sem=w_sem.at[0, at], recv_sem=w_sem.at[1, at],
+            src_ref=src, dst_ref=wraw.at[at], send_sem=w_sem.at[0, at], recv_sem=w_sem.at[1, at],
             device_id={"fsdp": to}, device_id_type=MESH)
 
-    far_copies = [weight_copy(src, 2 + i, across) for i, src in enumerate(kinds)]
-    near_copies = [weight_copy(src, i, twin) for i, src in enumerate(kinds)]
-    for copy in far_copies[:1] + near_copies:
+    own_loads = [pltpu.make_async_copy(src, wraw.at[4 * i], w_sem.at[0, 4 * i]) for i, src in enumerate(kinds)]
+    near_copies = [weight_copy(src, 4 * i + 1, twin) for i, src in enumerate(kinds)]
+    far_copies = [weight_copy(src, 4 * i + 2, across) for i, src in enumerate(kinds)]
+    pass_copies = [weight_copy(wraw.at[4 * i + 2], 4 * i + 3, twin) for i in range(3)]
+    for copy in far_copies[:1] + near_copies + own_loads:
         copy.start()
 
     head_of = iota((1, features), 1) // HEAD_DIM
@@ -360,6 +362,8 @@
         merged[0] = merged[0] + part * (1.0 - pick_row)
         merged[1] = merged[1] + part * pick_row
     attended = jnp.concatenate(merged, axis=0).astype(BF16)
+    far_copies[0].wait_recv()
+    pass_copies[0].start()
 
     side, per_side = vs // 2, owners // 2
 
@@ -429,48 +433,53 @@
             n_copy(k, share(owner), ve).wait_recv()
             h_copy(k, share(owner), ve).wait_recv()
 
-    def await_sends(k, carry):
-        m_copy(k, k, me).wait_send()
-        o_copy(k, k, me).wait_send()
-        t_copy(k, k, me).wait_send()
-        return carry
-
-    lax.fori_loop(1, fs, await_sends, 0)
-    y_copy.wait_send()
-    for step in range(zs):
-        for dy in range(2):
-            twin_copy(4 * step + 2 * dy).wait_send()
-    for step in range(last + 1):
-        for way in range(2):
+    def finish():
+        def await_sends(k, carry):
+            m_copy(k, k, me).wait_send()
+            o_copy(k, k, me).wait_send()
+            t_copy(k, k, me).wait_send()
+            return carry
+
+        lax.fori_loop(1, fs, await_sends, 0)
+        y_copy.wait_send()
+        for step in range(zs):
             for dy in range(2):
-                if step < last or way == dy:
-                    ring_copy(way, step, dy).wait_send()
-    for k in range(1, vs):
-        to = lax.rem(ve + k, vs)
-
-        @pl.when(owns(to))
-        def _():
-            p_copy(k, to).wait_send()
-
-    @pl.when(owns(ve))
-    def _():
+                twin_copy(4 * step + 2 * dy).wait_send()
+        for step in range(last + 1):
+            for way in range(2):
+                for dy in range(2):
+                    if step < last or way == dy:
+                        ring_copy(way, step, dy).wait_send()
         for k in range(1, vs):
             to = lax.rem(ve + k, vs)
-            n_copy(k, own, to).wait_send()
-            h_copy(k, own, to).wait_send()
-
-    for copy in far_copies + near_copies:
-        copy.wait()
-
-
-def expert_kernel(
-    fs, vs, zs,
-    normed_ref, cols_ref, routes_ref, router_ref, wg_ref, wu_ref, wd_ref, more_ref,
+
+            @pl.when(owns(to))
+            def _():
+                p_copy(k, to).wait_send()
+
+        @pl.when(owns(ve))
+        def _():
+            for k in range(1, vs):
+                to = lax.rem(ve + k, vs)
+                n_copy(k, own, to).wait_send()
+                h_copy(k, own, to).wait_send()
+
+        for copy in far_copies + near_copies + pass_copies:
+            copy.wait_send()
+
+    return finish, own_loads, near_copies, far_copies, pass_copies
+
+
+def expert_part(
+    fs, vs, zs, own_loads, near_copies, far_copies, pass_copies,
+    normed_ref, cols_ref, routes_ref, router_ref,
     out_ref,
     wraw, weights, rt_scr, xbuf, obuf, sbuf, rbuf, fsend, frecv,
-    w_sem, d_sem, p_sem, ag_sem, rs_sem, f_sem,
+    ag_sem, rs_sem, f_sem,
 ):
-    tokens, width = normed_ref.shape
+    owners, per_owner, width = normed_ref.shape
+    tokens = owners * per_owner
+    normed = normed_ref[...].reshape(tokens, width)
     block = xbuf.shape[1] // 2
     cut = xbuf.shape[2]
     slots = fsend.shape[1]
@@ -484,22 +493,6 @@
     yhi = me // (2 * zs)
     right = (yhi * zs + lax.rem(z + 1, zs)) * 2 + core
     left = (yhi * zs + lax.rem(z + zs - 1, zs)) * 2 + core
-    twin = me + 1 - 2 * core
-    across = lax.rem(me + fs // 2, fs)
-
-    barrier = pltpu.get_barrier_semaphore()
-    for peer in (left, right, twin, across):
-        pl.semaphore_signal(barrier, inc=1, device_id={"fsdp": peer}, device_id_type=MESH)
-    for k in range(1, vs):
-        pl.semaphore_signal(barrier, inc=1, device_id={"vocab": lax.rem(ve + k, vs)}, device_id_type=MESH)
-    loads = []
-    for i, src in enumerate((wg_ref, wu_ref, wd_ref)):
-        loads.append(pltpu.make_async_copy(src, wraw.at[i * sources], w_sem.at[i * sources]))
-        for j in range(1, sources - 1 if i < 2 else 1):
-            loads.append(pltpu.make_async_copy(
-                more_ref.at[(j - 1) * 2 + i], wraw.at[i * sources + j], w_sem.at[i * sources + j]))
-    for load in loads:
-        load.start()
 
     rt_scr[...] = jnp.zeros(rt_scr.shape, F32)
     rt_scr[0:2, 0:tokens] = routes_ref[...].astype(F32)
@@ -513,9 +506,8 @@
     my_rank = jnp.sum(jnp.where(lane == ve, ranks, 0.0), axis=1, keepdims=True)
     mine = jnp.where((my_hit > 0.5) & (my_rank == lane.astype(F32)), 1.0, 0.0)
 
-    picked = mm_tn(mine.astype(BF16), normed_ref[...])[0:block]
+    picked = mm_tn(mine.astype(BF16), normed)[0:block]
     xbuf[0] = jnp.concatenate([picked[:, 0:cut], picked[:, cut:width]], axis=0).astype(BF16)
-    pl.semaphore_wait(barrier, 4 + vs - 1)
 
     ways = (right, left)
     steps = zs // 2
@@ -562,26 +554,11 @@
                     obuf[first_block + i, side * block : (side + 1) * block, c * tile : (c + 1) * tile] = (
                         out[i * block : (i + 1) * block])
 
-    def down_copy(src, j, to):
-        return pltpu.make_async_remote_copy(
-            src_ref=src, dst_ref=wraw.at[2 * sources + j], send_sem=d_sem.at[0, j], recv_sem=d_sem.at[1, j],
-            device_id={"fsdp": to}, device_id_type=MESH)
-
-    down_far = down_copy(wd_ref, 2, across)
-    down_near = down_copy(wd_ref, 1, twin)
-    down_pass = down_copy(wraw.at[2 * sources + 2], 3, twin)
-    up_pass = [
-        pltpu.make_async_remote_copy(
-            src_ref=more_ref.at[2 + i], dst_ref=wraw.at[i * sources + 3],
-            send_sem=p_sem.at[0, i], recv_sem=p_sem.at[1, i], device_id={"fsdp": twin}, device_id_type=MESH)
-        for i in range(2)
-    ]
     gather_step(0)
-    for copy in up_pass:
-        copy.start()
-    down_far.start()
-    down_near.start()
-    logits = mm_nt(normed_ref[...], router_ref[...])
+    far_copies[2].start()
+    far_copies[1].wait_recv()
+    pass_copies[1].start()
+    logits = mm_nt(normed, router_ref[...])
     lane8 = iota(logits.shape, 1)
     chosen0 = jnp.sum(jnp.where(lane8 == first, logits, 0.0), axis=1, keepdims=True)
     chosen1 = jnp.sum(jnp.where(lane8 == second, logits, 0.0), axis=1, keepdims=True)
@@ -595,17 +572,19 @@
     slot_at = (iota((tokens, vs * slots), 1) % slots).astype(F32)
     back = jnp.where((all_hits > 0.5) & (all_ranks == slot_at), 1.0, 0.0).astype(BF16)
 
-    for load in loads:
-        load.wait()
-    for copy in up_pass:
-        copy.wait_recv()
-
     def settle(i, carry):
         weights[i, pitch - 16 : pitch, :] = jnp.zeros((16, width), BF16)
         weights[i, 0:hidden, :] = wraw[i]
         return carry
 
-    lax.fori_loop(0, 2 * sources, settle, 0)
+    for load, near in zip(own_loads, near_copies):
+        load.wait()
+        near.wait_recv()
+    pass_copies[0].wait_recv()
+    lax.fori_loop(0, sources, settle, 0)
+    lax.fori_loop(2 * sources, 2 * sources + 2, settle, 0)
+    pass_copies[1].wait_recv()
+    lax.fori_loop(sources, 2 * sources, settle, 0)
     for step in range(1, steps):
         gather_step(step)
         if step == 2:
@@ -613,11 +592,11 @@
     for way in range(2):
         gather_copy(way, steps - 1, way).wait_recv()
     far_acts = expert_up(5, 3)
-    down_far.wait_recv()
-    down_pass.start()
-    down_near.wait_recv()
-    down_pass.wait_recv()
-    lax.fori_loop(2 * sources, 3 * sources, settle, 0)
+    far_copies[2].wait_recv()
+    pass_copies[2].start()
+    lax.fori_loop(2 * sources + 2, 2 * sources + 3, settle, 0)
+    pass_copies[2].wait_recv()
+    lax.fori_loop(2 * sources + 3, 3 * sources, settle, 0)
     expert_down(far_acts, 5, 3)
 
     def sum_copy(way, step, h):
@@ -669,10 +648,8 @@
     for k in range(1, vs):
         f_copy(k, ve, lax.rem(ve - k + vs, vs)).wait_recv()
     mixture = mm(back, frecv[...].reshape(vs * slots, padded))
-    out_ref[...] = (cols_ref[...] + mixture)[:, 0:columns].astype(BF16)
-
-    for copy in (down_far, down_near, down_pass, *up_pass):
-        copy.wait_send()
+    out_ref[...] = (cols_ref[...].reshape(tokens, padded) + mixture)[:, 0:columns].astype(BF16)
+
     for step in range(steps):
         for way in range(2):
             for h in halves(step, way):
@@ -684,6 +661,22 @@
                     sum_copy(way, step, h).wait_send()
     for k in range(1, vs):
         f_copy(k, lax.rem(ve + k, vs), ve).wait_send()
+
+
+def layer_kernel(fs, vs, zs, *refs):
+    inputs, rest = refs[:12], refs[12:]
+    routes_ref, router_ref = rest[:2]
+    weight_refs, out_ref, rest = rest[2:5], rest[5], rest[6:]
+    normed_ref, cols_ref = rest[:2]
+    attention_scratch, expert_scratch, rest = rest[2:19], rest[19:28], rest[28:]
+    attention_sems, expert_sems = rest[:12], rest[12:]
+    finish, *copies = attention_part(
+        fs, vs, zs, *inputs, *weight_refs, expert_scratch[0], normed_ref, cols_ref,
+        *attention_scratch, *attention_sems)
+    expert_part(
+        fs, vs, zs, *copies, normed_ref, cols_ref, routes_ref, router_ref, out_ref,
+        *expert_scratch, *expert_sems)
+    finish()
 
 
 def per_device(
@@ -706,15 +699,15 @@
     per_owner = 16
     owners = tokens // per_owner
     wg, wu, wd = gate_weight[0].T, up_weight[0].T, down_weight[0]
-    normed, cols, more = pl.pallas_call(
-        functools.partial(attention_kernel, fs, vs, zs),
-        out_shape=(
-            jax.ShapeDtypeStruct((owners, per_owner, width), BF16),
-            jax.ShapeDtypeStruct((owners, per_owner, padded), F32),
-            jax.ShapeDtypeStruct((4, hidden, width), BF16)),
-        in_specs=[vmem] * 4 + [smem] * 2 + [vmem] * 4 + [hbm] * 4,
-        out_specs=(vmem, vmem, hbm),
+    block, slots = 40, 48
+    return pl.pallas_call(
+        functools.partial(layer_kernel, fs, vs, zs),
+        out_shape=jax.ShapeDtypeStruct((tokens, width // vs), BF16),
+        in_specs=[vmem] * 4 + [smem] * 2 + [vmem] * 4 + [hbm] * 2 + [vmem] * 2 + [hbm] * 3,
+        out_specs=vmem,
         scratch_shapes=[
+            pltpu.VMEM((owners, per_owner, width), BF16),
+            pltpu.VMEM((owners, per_owner, padded), F32),
             pltpu.VMEM(pool_keys.shape, BF16),
             pltpu.VMEM(pool_values.shape, BF16),
             pltpu.VMEM((pool_pages // 2, page_rows, 512), F32),
@@ -732,24 +725,6 @@
             pltpu.VMEM((owners, per_owner, width), BF16),
             pltpu.VMEM((vs, per_owner, width), BF16),
             pltpu.VMEM((vs, per_owner, padded), F32),
-            dma((4,)), dma((2, 4)), dma((fs,)), dma((1,)), dma((2, zs // 2, 2)), dma((fs // 2,)),
-            dma((2, fs)), dma((2, fs)), dma((2, fs)),
-            dma((2, vs)), dma((2, vs)), dma((2, vs)),
-        ],
-        compiler_params=pltpu.CompilerParams(
-            collective_id=1, has_side_effects=True, vmem_limit_bytes=56 * 2**20),
-        name="attention",
-    )(
-        queries, new_keys, new_values, page_table, cache_lengths, serve_pages.reshape(-1), parents,
-        resid.reshape(owners, per_owner, width), out_weight, norm_gain,
-        pool_keys, pool_values, wg, wu)
-    block, slots = 40, 48
-    return pl.pallas_call(
-        functools.partial(expert_kernel, fs, vs, zs),
-        out_shape=jax.ShapeDtypeStruct((tokens, width // vs), BF16),
-        in_specs=[vmem] * 4 + [hbm] * 4,
-        out_specs=vmem,
-        scratch_shapes=[
             pltpu.VMEM((12, hidden, width), BF16),
             pltpu.VMEM((12, pitch, width), BF16),
             pltpu.VMEM((128, 128), F32),
@@ -759,12 +734,17 @@
             pltpu.VMEM((2, zs // 2, 2 * block, width // 2), BF16),
             pltpu.VMEM((vs, slots, padded), BF16),
             pltpu.VMEM((vs, slots, padded), BF16),
-            dma((12,)), dma((2, 4)), dma((2, 2)), dma((2, 2, zs // 2, 2)), dma((2, 2, zs // 2, 2)), dma((2, vs)),
+            dma((4,)), dma((2, 12)), dma((fs,)), dma((1,)), dma((2, zs // 2, 2)), dma((fs // 2,)),
+            dma((2, fs)), dma((2, fs)), dma((2, fs)), dma((2, vs)), dma((2, vs)), dma((2, vs)),
+            dma((2, 2, zs // 2, 2)), dma((2, 2, zs // 2, 2)), dma((2, vs)),
         ],
         compiler_params=pltpu.CompilerParams(
-            collective_id=2, has_side_effects=True, vmem_limit_bytes=56 * 2**20),
-        name="experts",
-    )(normed.reshape(tokens, width), cols.reshape(tokens, padded), routes.T, router.T, wg, wu, wd, more)
+            collective_id=1, has_side_effects=True, vmem_limit_bytes=60 * 2**20),
+        name="layer",
+    )(
+        queries, new_keys, new_values, page_table, cache_lengths, serve_pages.reshape(-1), parents,
+        resid.reshape(owners, per_owner, width), out_weight, norm_gain, pool_keys, pool_values,
+        routes.T, router.T, wg, wu, wd)
 
 
 def solution(mesh):

time: 138 us -> 132 us (0.957)
  Pallas kernels: 136 us -> 130 us
    pallas_call x2 -> x1, Pallas kernels: 136 us -> 130 us  [per_device(): pl.pallas_call(functools.partial(layer_kernel, fs, vs, zs), out_shape=jax...]
where the time goes in v4:
time: 132 us
  Pallas kernels  130 us (98%)
  local copies, waits for them, and re-layouts  1.52 us (1%)
    pallas_call x1, Pallas kernels, per_device(): pl.pallas_call(functools.partial(layer_kernel, fs, vs, zs), out_shape=jax...  130 us

profile of v4, /device:TPU:32, one launch (start us, length us, event | category | flops | bytes accessed | tf_op | source)
XLA Modules:
  0.0 131.9 jit_solution(11591032602749161494)
XLA Ops:
  0.0 130.4 %layer.1 = bf16[96,288]{1,0:T(8,128)(2,1)} custom-call(bf16[96,256]{1,0:T(8,128)(2,1)} %refs_0_.1, bf16[96,256]{1,0:T(8,128)(2,1)} %refs_1_.1, bf16[96,256]{1,0:T(8,128)(2,1)} %refs_2_.1, s32[2,32]{1,0:T(2,128)} %refs_3_.1, s32[2]{0:T(128)} %refs_4_.1, s32[32]{0:T(128)} %bitcast.17, s32[2,48]{1,0:T(2,128)} %refs_6_.1, bf16[6,16,2304]{2,1,0:T(8,128)(2,1)} %bitcast.14, ...), custom_call_target="tpu_custom_call" | custom-call | tf_op jit(solution)/shard_map/layer/pallas_call | solution.py:703
  130.4 1.5 %copy.19 = bf16[96,288]{1,0:T(8,128)(2,1)} copy(bf16[96,288]{1,0:T(8,128)(2,1)} %layer.1) | data formatting | bytes 110592

commit v5 on v4

--- a/solution.py
+++ b/solution.py
@@ -35,7 +35,7 @@
 def attention_part(
     fs, vs, zs,
     q_ref, nk_ref, nv_ref, table_ref, length_ref, serve_ref, parent_ref, resid_ref, ow_ref, gain_ref,
-    pk_ref, pv_ref, wg_ref, wu_ref, wd_ref, wraw,
+    pk_ref, pv_ref, wg_ref, wu_ref, wd_ref, wraw, packed,
     normed_ref, cols_ref,
     kbuf, vbuf, s_scr, lim_scr, rq_scr, wt_scr, qall, msend, mrecv, osend, orecv, tsend, trecv,
     pown, psend, precv, hsend,
@@ -406,6 +406,18 @@
         def _():
             p_copy(k, to).start()
 
+    hidden_units, pitch = wraw.shape[1], packed.shape[1]
+
+    def settle(i, carry):
+        packed[i, pitch - 16 : pitch, :] = jnp.zeros((16, width), BF16)
+        packed[i, 0:hidden_units, :] = wraw[i]
+        return carry
+
+    for i in range(3):
+        own_loads[i].wait()
+        near_copies[i].wait_recv()
+        lax.fori_loop(4 * i, 4 * i + (3 if i == 0 else 2), settle, 0)
+
     @pl.when(owns(ve))
     def _():
         hidden = resid_ref[own].astype(F32) + pown[own]
@@ -425,13 +437,28 @@
             h_copy(k, own, lax.rem(ve + k, vs)).start()
         cols_ref[own] = hsend[ve]
 
+    pass_copies[0].wait_recv()
+    lax.fori_loop(3, 4, settle, 0)
+    far_copies[1].wait_recv()
+    pass_copies[1].start()
+    lax.fori_loop(6, 7, settle, 0)
+
     for k in range(1, vs):
         owner = lax.rem(ve - k + vs, vs)
 
         @pl.when(owns(owner))
         def _():
             n_copy(k, share(owner), ve).wait_recv()
-            h_copy(k, share(owner), ve).wait_recv()
+
+    far_copies[2].start()
+
+    def await_columns():
+        for k in range(1, vs):
+            owner = lax.rem(ve - k + vs, vs)
+
+            @pl.when(owns(owner))
+            def _():
+                h_copy(k, share(owner), ve).wait_recv()
 
     def finish():
         def await_sends(k, carry):
@@ -467,11 +494,11 @@
         for copy in far_copies + near_copies + pass_copies:
             copy.wait_send()
 
-    return finish, own_loads, near_copies, far_copies, pass_copies
+    return finish, await_columns, far_copies, pass_copies
 
 
 def expert_part(
-    fs, vs, zs, own_loads, near_copies, far_copies, pass_copies,
+    fs, vs, zs, await_columns, far_copies, pass_copies,
     normed_ref, cols_ref, routes_ref, router_ref,
     out_ref,
     wraw, weights, rt_scr, xbuf, obuf, sbuf, rbuf, fsend, frecv,
@@ -555,9 +582,6 @@
                         out[i * block : (i + 1) * block])
 
     gather_step(0)
-    far_copies[2].start()
-    far_copies[1].wait_recv()
-    pass_copies[1].start()
     logits = mm_nt(normed, router_ref[...])
     lane8 = iota(logits.shape, 1)
     chosen0 = jnp.sum(jnp.where(lane8 == first, logits, 0.0), axis=1, keepdims=True)
@@ -577,16 +601,11 @@
         weights[i, 0:hidden, :] = wraw[i]
         return carry
 
-    for load, near in zip(own_loads, near_copies):
-        load.wait()
-        near.wait_recv()
-    pass_copies[0].wait_recv()
-    lax.fori_loop(0, sources, settle, 0)
-    lax.fori_loop(2 * sources, 2 * sources + 2, settle, 0)
-    pass_copies[1].wait_recv()
-    lax.fori_loop(sources, 2 * sources, settle, 0)
     for step in range(1, steps):
         gather_step(step)
+        if step == 1:
+            pass_copies[1].wait_recv()
+            lax.fori_loop(2 * sources - 1, 2 * sources, settle, 0)
         if step == 2:
             near_acts = expert_up(0, 5)
     for way in range(2):
@@ -648,6 +667,7 @@
     for k in range(1, vs):
         f_copy(k, ve, lax.rem(ve - k + vs, vs)).wait_recv()
     mixture = mm(back, frecv[...].reshape(vs * slots, padded))
+    await_columns()
     out_ref[...] = (cols_ref[...].reshape(tokens, padded) + mixture)[:, 0:columns].astype(BF16)
 
     for step in range(steps):
@@ -671,7 +691,7 @@
     attention_scratch, expert_scratch, rest = rest[2:19], rest[19:28], rest[28:]
     attention_sems, expert_sems = rest[:12], rest[12:]
     finish, *copies = attention_part(
-        fs, vs, zs, *inputs, *weight_refs, expert_scratch[0], normed_ref, cols_ref,
+        fs, vs, zs, *inputs, *weight_refs, *expert_scratch[:2], normed_ref, cols_ref,
         *attention_scratch, *attention_sems)
     expert_part(
         fs, vs, zs, *copies, normed_ref, cols_ref, routes_ref, router_ref, out_ref,

time: 132 us -> 132 us (level)
  no operation moved by 1% of the time
where the time goes in v5:
time: 132 us; the launch traced here: 131 us
  Pallas kernels  130 us (98%)
  local copies, waits for them, and re-layouts  1.52 us (1%)
    pallas_call x1, Pallas kernels, per_device(): pl.pallas_call(functools.partial(layer_kernel, fs, vs, zs), out_shape=jax...  130 us

profile of v5, /device:TPU:32, one launch (start us, length us, event | category | flops | bytes accessed | tf_op | source)
XLA Modules:
  0.0 131.2 jit_solution(17635167921255370182)
XLA Ops:
  0.0 129.7 %layer.1 = bf16[96,288]{1,0:T(8,128)(2,1)} custom-call(bf16[96,256]{1,0:T(8,128)(2,1)} %refs_0_.1, bf16[96,256]{1,0:T(8,128)(2,1)} %refs_1_.1, bf16[96,256]{1,0:T(8,128)(2,1)} %refs_2_.1, s32[2,32]{1,0:T(2,128)} %refs_3_.1, s32[2]{0:T(128)} %refs_4_.1, s32[32]{0:T(128)} %bitcast.17, s32[2,48]{1,0:T(2,128)} %refs_6_.1, bf16[6,16,2304]{2,1,0:T(8,128)(2,1)} %bitcast.14, ...), custom_call_target="tpu_custom_call" | custom-call | tf_op jit(solution)/shard_map/layer/pallas_call | solution.py:723
  129.7 1.5 %copy.19 = bf16[96,288]{1,0:T(8,128)(2,1)} copy(bf16[96,288]{1,0:T(8,128)(2,1)} %layer.1) | data formatting | bytes 110592

commit v6 on v5

--- a/solution.py
+++ b/solution.py
@@ -608,9 +608,10 @@
             lax.fori_loop(2 * sources - 1, 2 * sources, settle, 0)
         if step == 2:
             near_acts = expert_up(0, 5)
+    third_acts = expert_up(5, 2)
     for way in range(2):
         gather_copy(way, steps - 1, way).wait_recv()
-    far_acts = expert_up(5, 3)
+    far_acts = jnp.concatenate([third_acts, expert_up(7, 1)], axis=0)
     far_copies[2].wait_recv()
     pass_copies[2].start()
     lax.fori_loop(2 * sources + 2, 2 * sources + 3, settle, 0)

time: 132 us -> 131 us (level)
  no operation moved by 1% of the time
where the time goes in v6:
time: 131 us
  Pallas kernels  129 us (98%)
  local copies, waits for them, and re-layouts  1.52 us (1%)
    pallas_call x1, Pallas kernels, per_device(): pl.pallas_call(functools.partial(layer_kernel, fs, vs, zs), out_shape=jax...  129 us

profile of v6, /device:TPU:32, one launch (start us, length us, event | category | flops | bytes accessed | tf_op | source)
XLA Modules:
  0.0 131.0 jit_solution(17987151082952598305)
XLA Ops:
  0.0 129.4 %layer.1 = bf16[96,288]{1,0:T(8,128)(2,1)} custom-call(bf16[96,256]{1,0:T(8,128)(2,1)} %refs_0_.1, bf16[96,256]{1,0:T(8,128)(2,1)} %refs_1_.1, bf16[96,256]{1,0:T(8,128)(2,1)} %refs_2_.1, s32[2,32]{1,0:T(2,128)} %refs_3_.1, s32[2]{0:T(128)} %refs_4_.1, s32[32]{0:T(128)} %bitcast.17, s32[2,48]{1,0:T(2,128)} %refs_6_.1, bf16[6,16,2304]{2,1,0:T(8,128)(2,1)} %bitcast.14, ...), custom_call_target="tpu_custom_call" | custom-call | tf_op jit(solution)/shard_map/layer/pallas_call | solution.py:724
  129.5 1.5 %copy.19 = bf16[96,288]{1,0:T(8,128)(2,1)} copy(bf16[96,288]{1,0:T(8,128)(2,1)} %layer.1) | data formatting | bytes 110592
